TPU v7x, 256 devices: a whole 4x4x8 slice. The times are simulated.
256 devices in a mesh: gx: 16 (over x, y), gy: 16 (over z, core).
Axes of the slice: x: 4, y: 4, z: 8, core: 2. Of those that a mesh axis runs over, the one named last changes fastest.
Arguments:
- members: float32 [4, 2048, 2048], P(None, 'gy', 'gx'), may hold values from -6 to 6
- analysis: float32 [2048, 2048], P('gy', 'gx'), may hold values from -6 to 6
- land_sea: int32 [2048, 2048], P('gy', 'gx'), may hold values 0 or 1
Outputs:
- member_grad: float32 [4, 2048, 2048], P(None, 'gy', 'gx')
All inputs are finite; a program needn't handle non-finite values. No bound on the sum of `land_sea` on one device may be relied on, other than what follows from the above.
Results may differ from a plain program's by a relative error of at most 0.00002.
Values sent between devices are 32-bit elements; how exact they have to be, the bound alone decides.
A program may use at most 64 MiB of HBM per device.

v0:
```python
import jax
import jax.numpy as jnp
from jax import lax
from jax.sharding import PartitionSpec as P

H1 = 4
H2 = 16
H3 = 64


smooth_sq = 0.01


def extended_2(block, sides, width):
    for axis, dim in sides:
        count = lax.axis_size(axis)
        forward = [(i, i + 1) for i in range(count - 1)]
        backward = [(target, source) for source, target in forward]
        low = lax.ppermute(
            lax.slice_in_dim(block, block.shape[dim] - width, None, axis=dim), axis, forward
        )
        high = lax.ppermute(lax.slice_in_dim(block, 0, width, axis=dim), axis, backward)
        block = jnp.concatenate([low, block, high], axis=dim)
    return block


def box_sum(field, radius, along):
    length = field.shape[along] - 2 * radius
    running = jnp.cumsum(field, axis=along)
    leading = jnp.zeros_like(lax.slice_in_dim(running, 0, 1, axis=along))
    running = jnp.concatenate([leading, running], axis=along)
    upper = lax.slice_in_dim(running, 2 * radius + 1, 2 * radius + 1 + length, axis=along)
    lower = lax.slice_in_dim(running, 0, length, axis=along)
    return upper - lower


def pool(field, radius):
    return box_sum(box_sum(field, radius, 1), radius, 2) / (2 * radius + 1)


def slope_of(gap_value):
    return gap_value * lax.rsqrt(gap_value * gap_value + smooth_sq)


def score_slope(pooled, truth, weight):
    count = pooled.shape[0]
    own_slope = slope_of(pooled - truth[None])
    spread = [jnp.zeros_like(pooled[0]) for member in range(count)]
    for first in range(count):
        for second in range(first + 1, count):
            paired = slope_of(pooled[first] - pooled[second])
            spread[first] = spread[first] + paired
            spread[second] = spread[second] - paired
    spread_all = jnp.stack(spread, axis=0)
    return weight[None] * (own_slope / count - spread_all / (count * (count - 1)))


def local(members, analysis, land_sea):
    count = members.shape[0]
    weight = land_sea.astype(jnp.float32)
    fields = jnp.concatenate([members, analysis[None]], axis=0)
    factor = 1
    gradient_sum = jnp.zeros_like(members)
    for radius in (H1, H2, H3):
        reach = factor * radius
        extended = extended_2(fields, (("gx", 2), ("gy", 1)), reach)
        pooled = pool(extended, radius)
        slope_map = score_slope(pooled[:count], pooled[count], weight)
        widened = extended_2(slope_map, (("gx", 2), ("gy", 1)), radius)
        gradient_sum = gradient_sum + pool(widened, radius)
    return gradient_sum


def solution(mesh):
    return jax.shard_map(
        local,
        mesh=mesh,
        in_specs=(P(None, "gy", "gx"), P("gy", "gx"), P("gy", "gx")),
        out_specs=P(None, "gy", "gx"),
        check_vma=False,
    )
```

profile of v0, /device:TPU:99, one launch (start us, length us, event | category | flops | bytes accessed | tf_op | source)
XLA Modules:
  0.0 154.5 jit_solution(12427959657398601808)
XLA Ops:
  1.3 3.2 %collective-permute-start = (f32[5,128,4]{2,1,0:T(8,128)S(1)}, f32[5,128,4]{2,1,0:T(8,128)S(1)}, u32[]{:S(2)}, u32[]{:S(2)}) collective-permute-start(f32[5,128,4]{2,1,0:T(8,128)S(1)} %get-tuple-element.34), channel_id=1, source_target_pairs={{0,16},{16,32},{32,48},{48,64},{64,80},{80,96},{96,112},{112,128},... | collective-permute-start | bytes 30728 | tf_op jit(solution)/shard_map/ppermute | solution.py:19
  4.5 4.3 %collective-permute-start.1 = (f32[5,128,4]{2,1,0:T(8,128)S(1)}, f32[5,128,4]{2,1,0:T(8,128)S(1)}, u32[]{:S(2)}, u32[]{:S(2)}) collective-permute-start(f32[5,128,4]{2,1,0:T(8,128)S(1)} %get-tuple-element.35), channel_id=1, source_target_pairs={{16,0},{32,16},{48,32},{64,48},{80,64},{96,80},{112,96},{128,112},... | collective-permute-start | bytes 30728 | tf_op jit(solution)/shard_map/ppermute | solution.py:22
  8.8 2.0 %fusion.29 = (f32[5,128,16]{2,1,0:T(8,128)}, f32[5,128,16]{2,1,0:T(8,128)}) fusion(f32[4,128,128]{2,1,0:T(8,128)} %param.3, f32[1,128,128]{2,1,0:T(8,128)} %bitcast.78), kind=kLoop, calls=%fused_computation.64 | loop fusion | flops 20480 | bytes 409600 | tf_op jit(solution)/shard_map/concatenate | solution.py:61
  10.8 1.9 %collective-permute-start.8 = (f32[5,128,16]{2,1,0:T(8,128)}, f32[5,128,16]{2,1,0:T(8,128)S(1)}, u32[]{:S(2)}, u32[]{:S(2)}) collective-permute-start(f32[5,128,16]{2,1,0:T(8,128)} %get-tuple-element.27), channel_id=1, source_target_pairs={{0,16},{16,32},{32,48},{48,64},{64,80},{80,96},{96,112},{112,128},... | collective-permute-start | bytes 122888 | tf_op jit(solution)/shard_map/ppermute | solution.py:19
  12.7 5.5 %collective-permute-start.9 = (f32[5,128,16]{2,1,0:T(8,128)}, f32[5,128,16]{2,1,0:T(8,128)}, u32[]{:S(2)}, u32[]{:S(2)}) collective-permute-start(f32[5,128,16]{2,1,0:T(8,128)} %get-tuple-element.28), channel_id=1, source_target_pairs={{16,0},{32,16},{48,32},{64,48},{80,64},{96,80},{112,96},{128,112},... | collective-permute-start | bytes 122888 | tf_op jit(solution)/shard_map/ppermute | solution.py:22
  18.3 6.4 %collective-permute-start.2 = (f32[5,4,136]{2,1,0:T(4,128)S(1)}, f32[5,4,136]{2,1,0:T(4,128)S(1)}, u32[]{:S(2)}, u32[]{:S(2)}) collective-permute-start(f32[5,4,136]{2,1,0:T(4,128)S(1)} %get-tuple-element.7), channel_id=1, source_target_pairs={{0,1},{1,2},{2,3},{3,4},{4,5},{5,6},{6,7},{7,8},{8,9},{9,10},{10,1... | collective-permute-start | bytes 32648 | tf_op jit(solution)/shard_map/ppermute | solution.py:19
  24.8 1.9 %collective-permute-start.3 = (f32[5,4,136]{2,1,0:T(4,128)S(1)}, f32[5,4,136]{2,1,0:T(4,128)S(1)}, u32[]{:S(2)}, u32[]{:S(2)}) collective-permute-start(f32[5,4,136]{2,1,0:T(4,128)S(1)} %get-tuple-element.8), channel_id=1, source_target_pairs={{1,0},{2,1},{3,2},{4,3},{5,4},{6,5},{7,6},{8,7},{9,8},{10,9},{11,1... | collective-permute-start | bytes 32648 | tf_op jit(solution)/shard_map/ppermute | solution.py:22
  27.7 1.9 %collective-permute-start.16 = (f32[5,128,64]{2,1,0:T(8,128)}, f32[5,128,64]{2,1,0:T(8,128)}, u32[]{:S(2)}, u32[]{:S(2)}) collective-permute-start(f32[5,128,64]{2,1,0:T(8,128)} %get-tuple-element.18), channel_id=1, source_target_pairs={{0,16},{16,32},{32,48},{48,64},{64,80},{80,96},{96,112},{112,128},... | collective-permute-start | bytes 491528 | tf_op jit(solution)/shard_map/ppermute | solution.py:19
  29.7 5.5 %collective-permute-start.17 = (f32[5,128,64]{2,1,0:T(8,128)}, f32[5,128,64]{2,1,0:T(8,128)}, u32[]{:S(2)}, u32[]{:S(2)}) collective-permute-start(f32[5,128,64]{2,1,0:T(8,128)} %get-tuple-element.19), channel_id=1, source_target_pairs={{16,0},{32,16},{48,32},{64,48},{80,64},{96,80},{112,96},{128,112},... | collective-permute-start | bytes 491528 | tf_op jit(solution)/shard_map/ppermute | solution.py:22
  37.2 2.4 %copy.9 = f32[5,136,2,128]{3,2,1,0:T(2,128)} copy(f32[5,136,2,128]{1,2,3,0:T(2,128)S(1)} %broadcast_add_fusion.2) | data formatting | bytes 1392640 | tf_op jit(solution)/shard_map/reduce_window_sum
  43.2 5.4 %collective-permute-start.10 = (f32[5,16,160]{2,1,0:T(8,128)S(1)}, f32[5,16,160]{2,1,0:T(8,128)S(1)}, u32[]{:S(2)}, u32[]{:S(2)}) collective-permute-start(f32[5,16,160]{2,1,0:T(8,128)S(1)} %get-tuple-element.5), channel_id=1, source_target_pairs={{0,1},{1,2},{2,3},{3,4},{4,5},{5,6},{6,7},{7,8},{8,9},{9,10},{10,1... | collective-permute-start | bytes 153608 | tf_op jit(solution)/shard_map/ppermute | solution.py:19
  48.7 1.9 %collective-permute-start.11 = (f32[5,16,160]{2,1,0:T(8,128)S(1)}, f32[5,16,160]{2,1,0:T(8,128)S(1)}, u32[]{:S(2)}, u32[]{:S(2)}) collective-permute-start(f32[5,16,160]{2,1,0:T(8,128)S(1)} %get-tuple-element.6), channel_id=1, source_target_pairs={{1,0},{2,1},{3,2},{4,3},{5,4},{6,5},{7,6},{8,7},{9,8},{10,9},{11,1... | collective-permute-start | bytes 153608 | tf_op jit(solution)/shard_map/ppermute | solution.py:22
  51.7 3.9 %collective-permute-done.11 = f32[5,16,160]{2,1,0:T(8,128)S(1)} collective-permute-done((f32[5,16,160]{2,1,0:T(8,128)S(1)}, f32[5,16,160]{2,1,0:T(8,128)S(1)}, u32[]{:S(2)}, u32[]{:S(2)}) %collective-permute-start.11) | collective-permute-done | bytes 51232 | tf_op jit(solution)/shard_map/ppermute | solution.py:22
  58.7 2.4 %copy.17 = f32[5,160,2,128]{3,2,1,0:T(2,128)} copy(f32[5,160,2,128]{1,2,3,0:T(2,128)S(1)} %broadcast_add_fusion.1) | data formatting | bytes 1638400 | tf_op jit(solution)/shard_map/reduce_window_sum
  66.7 1.9 %collective-permute-start.18 = (f32[5,64,256]{2,1,0:T(8,128)S(1)}, f32[5,64,256]{2,1,0:T(8,128)S(1)}, u32[]{:S(2)}, u32[]{:S(2)}) collective-permute-start(f32[5,64,256]{2,1,0:T(8,128)S(1)} %get-tuple-element.9), channel_id=1, source_target_pairs={{0,1},{1,2},{2,3},{3,4},{4,5},{5,6},{6,7},{7,8},{8,9},{9,10},{10,1... | collective-permute-start | bytes 983048 | tf_op jit(solution)/shard_map/ppermute | solution.py:19
  68.6 2.6 %collective-permute-start.19 = (f32[5,64,256]{2,1,0:T(8,128)S(1)}, f32[5,64,256]{2,1,0:T(8,128)S(1)}, u32[]{:S(2)}, u32[]{:S(2)}) collective-permute-start(f32[5,64,256]{2,1,0:T(8,128)S(1)} %get-tuple-element.10), channel_id=1, source_target_pairs={{1,0},{2,1},{3,2},{4,3},{5,4},{6,5},{7,6},{8,7},{9,8},{10,9},{11,1... | collective-permute-start | bytes 983048 | tf_op jit(solution)/shard_map/ppermute | solution.py:22
  72.6 5.6 %collective-permute-done.19 = f32[5,64,256]{2,1,0:T(8,128)S(1)} collective-permute-done((f32[5,64,256]{2,1,0:T(8,128)S(1)}, f32[5,64,256]{2,1,0:T(8,128)S(1)}, u32[]{:S(2)}, u32[]{:S(2)}) %collective-permute-start.19) | collective-permute-done | bytes 327712 | tf_op jit(solution)/shard_map/ppermute | solution.py:22
  83.0 1.9 %collective-permute-start.4 = (f32[4,128,4]{1,2,0:T(4,128)S(1)}, f32[4,128,4]{1,2,0:T(4,128)S(1)}, u32[]{:S(2)}, u32[]{:S(2)}) collective-permute-start(f32[4,128,4]{1,2,0:T(4,128)S(1)} %get-tuple-element.42), channel_id=1, source_target_pairs={{0,16},{16,32},{32,48},{48,64},{64,80},{80,96},{96,112},{112,128},... | collective-permute-start | bytes 24584 | tf_op jit(solution)/shard_map/ppermute | solution.py:19
  84.9 5.5 %collective-permute-start.5 = (f32[4,128,4]{1,2,0:T(4,128)S(1)}, f32[4,128,4]{1,2,0:T(4,128)S(1)}, u32[]{:S(2)}, u32[]{:S(2)}) collective-permute-start(f32[4,128,4]{1,2,0:T(4,128)S(1)} %get-tuple-element.43), channel_id=1, source_target_pairs={{16,0},{32,16},{48,32},{64,48},{80,64},{96,80},{112,96},{128,112},... | collective-permute-start | bytes 24584 | tf_op jit(solution)/shard_map/ppermute | solution.py:22
  91.1 1.9 %collective-permute-start.20 = (f32[4,128,64]{1,2,0:T(8,128)}, f32[4,128,64]{1,2,0:T(8,128)S(1)}, u32[]{:S(2)}, u32[]{:S(2)}) collective-permute-start(f32[4,128,64]{1,2,0:T(8,128)} %get-tuple-element.38), channel_id=1, source_target_pairs={{0,16},{16,32},{32,48},{48,64},{64,80},{80,96},{96,112},{112,128},... | collective-permute-start | bytes 393224 | tf_op jit(solution)/shard_map/ppermute | solution.py:19
  93.0 5.5 %collective-permute-start.21 = (f32[4,128,64]{1,2,0:T(8,128)}, f32[4,128,64]{1,2,0:T(8,128)S(1)}, u32[]{:S(2)}, u32[]{:S(2)}) collective-permute-start(f32[4,128,64]{1,2,0:T(8,128)} %get-tuple-element.39), channel_id=1, source_target_pairs={{16,0},{32,16},{48,32},{64,48},{80,64},{96,80},{112,96},{128,112},... | collective-permute-start | bytes 393224 | tf_op jit(solution)/shard_map/ppermute | solution.py:22
  98.7 2.9 %collective-permute-start.6 = (f32[4,4,136]{1,2,0:T(8,128)S(1)}, f32[4,4,136]{1,2,0:T(8,128)S(1)}, u32[]{:S(2)}, u32[]{:S(2)}) collective-permute-start(f32[4,4,136]{1,2,0:T(8,128)S(1)} %get-tuple-element.36), channel_id=1, source_target_pairs={{0,1},{1,2},{2,3},{3,4},{4,5},{5,6},{6,7},{7,8},{8,9},{9,10},{10,1... | collective-permute-start | bytes 26120 | tf_op jit(solution)/shard_map/ppermute | solution.py:19
  101.6 1.9 %collective-permute-start.7 = (f32[4,4,136]{1,2,0:T(8,128)S(1)}, f32[4,4,136]{1,2,0:T(8,128)S(1)}, u32[]{:S(2)}, u32[]{:S(2)}) collective-permute-start(f32[4,4,136]{1,2,0:T(8,128)S(1)} %get-tuple-element.37), channel_id=1, source_target_pairs={{1,0},{2,1},{3,2},{4,3},{5,4},{6,5},{7,6},{8,7},{9,8},{10,9},{11,1... | collective-permute-start | bytes 26120 | tf_op jit(solution)/shard_map/ppermute | solution.py:22
  104.1 1.9 %collective-permute-start.12 = (f32[4,128,16]{1,2,0:T(8,128)}, f32[4,128,16]{1,2,0:T(8,128)S(1)}, u32[]{:S(2)}, u32[]{:S(2)}) collective-permute-start(f32[4,128,16]{1,2,0:T(8,128)} %get-tuple-element.40), channel_id=1, source_target_pairs={{0,16},{16,32},{32,48},{48,64},{64,80},{80,96},{96,112},{112,128},... | collective-permute-start | bytes 98312 | tf_op jit(solution)/shard_map/ppermute | solution.py:19
  106.0 5.5 %collective-permute-start.13 = (f32[4,128,16]{1,2,0:T(8,128)S(1)}, f32[4,128,16]{1,2,0:T(8,128)S(1)}, u32[]{:S(2)}, u32[]{:S(2)}) collective-permute-start(f32[4,128,16]{1,2,0:T(8,128)S(1)} %get-tuple-element.41), channel_id=1, source_target_pairs={{16,0},{32,16},{48,32},{64,48},{80,64},{96,80},{112,96},{128,112},... | collective-permute-start | bytes 98312 | tf_op jit(solution)/shard_map/ppermute | solution.py:22
  115.8 5.4 %collective-permute-start.14 = (f32[4,16,160]{1,2,0:T(8,128)S(1)}, f32[4,16,160]{1,2,0:T(8,128)S(1)}, u32[]{:S(2)}, u32[]{:S(2)}) collective-permute-start(f32[4,16,160]{1,2,0:T(8,128)S(1)} %get-tuple-element.20), channel_id=1, source_target_pairs={{0,1},{1,2},{2,3},{3,4},{4,5},{5,6},{6,7},{7,8},{8,9},{9,10},{10,1... | collective-permute-start | bytes 122888 | tf_op jit(solution)/shard_map/ppermute | solution.py:19
  121.2 1.9 %collective-permute-start.15 = (f32[4,16,160]{1,2,0:T(8,128)S(1)}, f32[4,16,160]{1,2,0:T(8,128)S(1)}, u32[]{:S(2)}, u32[]{:S(2)}) collective-permute-start(f32[4,16,160]{1,2,0:T(8,128)S(1)} %get-tuple-element.21), channel_id=1, source_target_pairs={{1,0},{2,1},{3,2},{4,3},{5,4},{6,5},{7,6},{8,7},{9,8},{10,9},{11,1... | collective-permute-start | bytes 122888 | tf_op jit(solution)/shard_map/ppermute | solution.py:22
  125.2 5.6 %collective-permute-done.15 = f32[4,16,160]{1,2,0:T(8,128)S(1)} collective-permute-done((f32[4,16,160]{1,2,0:T(8,128)S(1)}, f32[4,16,160]{1,2,0:T(8,128)S(1)}, u32[]{:S(2)}, u32[]{:S(2)}) %collective-permute-start.15) | collective-permute-done | bytes 40992 | tf_op jit(solution)/shard_map/ppermute | solution.py:22
  135.8 1.9 %collective-permute-start.22 = (f32[4,64,256]{1,2,0:T(8,128)S(1)}, f32[4,64,256]{1,2,0:T(8,128)S(1)}, u32[]{:S(2)}, u32[]{:S(2)}) collective-permute-start(f32[4,64,256]{1,2,0:T(8,128)S(1)} %get-tuple-element.11), channel_id=1, source_target_pairs={{0,1},{1,2},{2,3},{3,4},{4,5},{5,6},{6,7},{7,8},{8,9},{9,10},{10,1... | collective-permute-start | bytes 786440 | tf_op jit(solution)/shard_map/ppermute | solution.py:19
  137.7 2.6 %collective-permute-start.23 = (f32[4,64,256]{1,2,0:T(8,128)S(1)}, f32[4,64,256]{1,2,0:T(8,128)S(1)}, u32[]{:S(2)}, u32[]{:S(2)}) collective-permute-start(f32[4,64,256]{1,2,0:T(8,128)S(1)} %get-tuple-element.12), channel_id=1, source_target_pairs={{1,0},{2,1},{3,2},{4,3},{5,4},{6,5},{7,6},{8,7},{9,8},{10,9},{11,1... | collective-permute-start | bytes 786440 | tf_op jit(solution)/shard_map/ppermute | solution.py:22
  140.7 3.1 %collective-permute-done.22 = f32[4,64,256]{1,2,0:T(8,128)S(1)} collective-permute-done((f32[4,64,256]{1,2,0:T(8,128)S(1)}, f32[4,64,256]{1,2,0:T(8,128)S(1)}, u32[]{:S(2)}, u32[]{:S(2)}) %collective-permute-start.22) | collective-permute-done | bytes 262176 | tf_op jit(solution)/shard_map/ppermute | solution.py:19
  143.8 5.6 %collective-permute-done.23 = f32[4,64,256]{1,2,0:T(8,128)S(1)} collective-permute-done((f32[4,64,256]{1,2,0:T(8,128)S(1)}, f32[4,64,256]{1,2,0:T(8,128)S(1)}, u32[]{:S(2)}, u32[]{:S(2)}) %collective-permute-start.23) | collective-permute-done | bytes 262176 | tf_op jit(solution)/shard_map/ppermute | solution.py:22
  (179 shorter events, 41.6 us)
Async XLA Ops:
  0.0 18.2 %copy-start.1 = (f32[128,128]{1,0:T(8,128)S(1)}, f32[128,128]{1,0:T(8,128)}, u32[]{:S(2)}) copy-start(f32[128,128]{1,0:T(8,128)} %param.4) | copy-start | bytes 196612
  0.0 18.2 %copy-start = (f32[4,128,128]{2,1,0:T(8,128)S(1)}, f32[4,128,128]{2,1,0:T(8,128)}, u32[]{:S(2)}) copy-start(f32[4,128,128]{2,1,0:T(8,128)} %param.3) | copy-start | bytes 786436
  1.3 16.9 %collective-permute-start = (f32[5,128,4]{2,1,0:T(8,128)S(1)}, f32[5,128,4]{2,1,0:T(8,128)S(1)}, u32[]{:S(2)}, u32[]{:S(2)}) collective-permute-start(f32[5,128,4]{2,1,0:T(8,128)S(1)} %get-tuple-element.34), channel_id=1, source_target_pairs={{0,16},{16,32},{32,48},{48,64},{64,80},{80,96},{96,112},{112,128},... | collective-permute-start | bytes 30728 | tf_op jit(solution)/shard_map/ppermute | solution.py:19
  4.5 25.1 %copy-start.14 = (s32[128,128]{1,0:T(8,128)S(1)}, s32[128,128]{1,0:T(8,128)}, u32[]{:S(2)}) copy-start(s32[128,128]{1,0:T(8,128)} %param.5) | copy-start | bytes 196612
  4.5 13.7 %collective-permute-start.1 = (f32[5,128,4]{2,1,0:T(8,128)S(1)}, f32[5,128,4]{2,1,0:T(8,128)S(1)}, u32[]{:S(2)}, u32[]{:S(2)}) collective-permute-start(f32[5,128,4]{2,1,0:T(8,128)S(1)} %get-tuple-element.35), channel_id=1, source_target_pairs={{16,0},{32,16},{48,32},{64,48},{80,64},{96,80},{112,96},{128,112},... | collective-permute-start | bytes 30728 | tf_op jit(solution)/shard_map/ppermute | solution.py:22
  10.8 31.4 %collective-permute-start.8 = (f32[5,128,16]{2,1,0:T(8,128)}, f32[5,128,16]{2,1,0:T(8,128)S(1)}, u32[]{:S(2)}, u32[]{:S(2)}) collective-permute-start(f32[5,128,16]{2,1,0:T(8,128)} %get-tuple-element.27), channel_id=1, source_target_pairs={{0,16},{16,32},{32,48},{48,64},{64,80},{80,96},{96,112},{112,128},... | collective-permute-start | bytes 122888 | tf_op jit(solution)/shard_map/ppermute | solution.py:19
  12.7 29.5 %collective-permute-start.9 = (f32[5,128,16]{2,1,0:T(8,128)}, f32[5,128,16]{2,1,0:T(8,128)}, u32[]{:S(2)}, u32[]{:S(2)}) collective-permute-start(f32[5,128,16]{2,1,0:T(8,128)} %get-tuple-element.28), channel_id=1, source_target_pairs={{16,0},{32,16},{48,32},{64,48},{80,64},{96,80},{112,96},{128,112},... | collective-permute-start | bytes 122888 | tf_op jit(solution)/shard_map/ppermute | solution.py:22
  18.3 11.4 %collective-permute-start.2 = (f32[5,4,136]{2,1,0:T(4,128)S(1)}, f32[5,4,136]{2,1,0:T(4,128)S(1)}, u32[]{:S(2)}, u32[]{:S(2)}) collective-permute-start(f32[5,4,136]{2,1,0:T(4,128)S(1)} %get-tuple-element.7), channel_id=1, source_target_pairs={{0,1},{1,2},{2,3},{3,4},{4,5},{5,6},{6,7},{7,8},{8,9},{9,10},{10,1... | collective-permute-start | bytes 32648 | tf_op jit(solution)/shard_map/ppermute | solution.py:19
  24.8 10.4 %collective-permute-start.3 = (f32[5,4,136]{2,1,0:T(4,128)S(1)}, f32[5,4,136]{2,1,0:T(4,128)S(1)}, u32[]{:S(2)}, u32[]{:S(2)}) collective-permute-start(f32[5,4,136]{2,1,0:T(4,128)S(1)} %get-tuple-element.8), channel_id=1, source_target_pairs={{1,0},{2,1},{3,2},{4,3},{5,4},{6,5},{7,6},{8,7},{9,8},{10,9},{11,1... | collective-permute-start | bytes 32648 | tf_op jit(solution)/shard_map/ppermute | solution.py:22
  27.7 37.5 %collective-permute-start.16 = (f32[5,128,64]{2,1,0:T(8,128)}, f32[5,128,64]{2,1,0:T(8,128)}, u32[]{:S(2)}, u32[]{:S(2)}) collective-permute-start(f32[5,128,64]{2,1,0:T(8,128)} %get-tuple-element.18), channel_id=1, source_target_pairs={{0,16},{16,32},{32,48},{48,64},{64,80},{80,96},{96,112},{112,128},... | collective-permute-start | bytes 491528 | tf_op jit(solution)/shard_map/ppermute | solution.py:19
  29.7 35.5 %collective-permute-start.17 = (f32[5,128,64]{2,1,0:T(8,128)}, f32[5,128,64]{2,1,0:T(8,128)}, u32[]{:S(2)}, u32[]{:S(2)}) collective-permute-start(f32[5,128,64]{2,1,0:T(8,128)} %get-tuple-element.19), channel_id=1, source_target_pairs={{16,0},{32,16},{48,32},{64,48},{80,64},{96,80},{112,96},{128,112},... | collective-permute-start | bytes 491528 | tf_op jit(solution)/shard_map/ppermute | solution.py:22
  42.2 8.7 %copy-start.8 = (f32[5,128,16]{2,1,0:T(8,128)}, f32[5,128,16]{2,1,0:T(8,128)S(1)}, u32[]{:S(2)}) copy-start(f32[5,128,16]{2,1,0:T(8,128)S(1)} %collective-permute-done.8) | copy-start | bytes 122884
  43.2 7.7 %collective-permute-start.10 = (f32[5,16,160]{2,1,0:T(8,128)S(1)}, f32[5,16,160]{2,1,0:T(8,128)S(1)}, u32[]{:S(2)}, u32[]{:S(2)}) collective-permute-start(f32[5,16,160]{2,1,0:T(8,128)S(1)} %get-tuple-element.5), channel_id=1, source_target_pairs={{0,1},{1,2},{2,3},{3,4},{4,5},{5,6},{6,7},{7,8},{8,9},{9,10},{10,1... | collective-permute-start | bytes 153608 | tf_op jit(solution)/shard_map/ppermute | solution.py:19
  48.7 7.0 %collective-permute-start.11 = (f32[5,16,160]{2,1,0:T(8,128)S(1)}, f32[5,16,160]{2,1,0:T(8,128)S(1)}, u32[]{:S(2)}, u32[]{:S(2)}) collective-permute-start(f32[5,16,160]{2,1,0:T(8,128)S(1)} %get-tuple-element.6), channel_id=1, source_target_pairs={{1,0},{2,1},{3,2},{4,3},{5,4},{6,5},{7,6},{8,7},{9,8},{10,9},{11,1... | collective-permute-start | bytes 153608 | tf_op jit(solution)/shard_map/ppermute | solution.py:22
  66.7 5.9 %collective-permute-start.18 = (f32[5,64,256]{2,1,0:T(8,128)S(1)}, f32[5,64,256]{2,1,0:T(8,128)S(1)}, u32[]{:S(2)}, u32[]{:S(2)}) collective-permute-start(f32[5,64,256]{2,1,0:T(8,128)S(1)} %get-tuple-element.9), channel_id=1, source_target_pairs={{0,1},{1,2},{2,3},{3,4},{4,5},{5,6},{6,7},{7,8},{8,9},{9,10},{10,1... | collective-permute-start | bytes 983048 | tf_op jit(solution)/shard_map/ppermute | solution.py:19
  68.6 9.6 %collective-permute-start.19 = (f32[5,64,256]{2,1,0:T(8,128)S(1)}, f32[5,64,256]{2,1,0:T(8,128)S(1)}, u32[]{:S(2)}, u32[]{:S(2)}) collective-permute-start(f32[5,64,256]{2,1,0:T(8,128)S(1)} %get-tuple-element.10), channel_id=1, source_target_pairs={{1,0},{2,1},{3,2},{4,3},{5,4},{6,5},{7,6},{8,7},{9,8},{10,9},{11,1... | collective-permute-start | bytes 983048 | tf_op jit(solution)/shard_map/ppermute | solution.py:22
  83.0 15.5 %collective-permute-start.4 = (f32[4,128,4]{1,2,0:T(4,128)S(1)}, f32[4,128,4]{1,2,0:T(4,128)S(1)}, u32[]{:S(2)}, u32[]{:S(2)}) collective-permute-start(f32[4,128,4]{1,2,0:T(4,128)S(1)} %get-tuple-element.42), channel_id=1, source_target_pairs={{0,16},{16,32},{32,48},{48,64},{64,80},{80,96},{96,112},{112,128},... | collective-permute-start | bytes 24584 | tf_op jit(solution)/shard_map/ppermute | solution.py:19
  84.9 13.6 %collective-permute-start.5 = (f32[4,128,4]{1,2,0:T(4,128)S(1)}, f32[4,128,4]{1,2,0:T(4,128)S(1)}, u32[]{:S(2)}, u32[]{:S(2)}) collective-permute-start(f32[4,128,4]{1,2,0:T(4,128)S(1)} %get-tuple-element.43), channel_id=1, source_target_pairs={{16,0},{32,16},{48,32},{64,48},{80,64},{96,80},{112,96},{128,112},... | collective-permute-start | bytes 24584 | tf_op jit(solution)/shard_map/ppermute | solution.py:22
  91.1 44.0 %collective-permute-start.20 = (f32[4,128,64]{1,2,0:T(8,128)}, f32[4,128,64]{1,2,0:T(8,128)S(1)}, u32[]{:S(2)}, u32[]{:S(2)}) collective-permute-start(f32[4,128,64]{1,2,0:T(8,128)} %get-tuple-element.38), channel_id=1, source_target_pairs={{0,16},{16,32},{32,48},{48,64},{64,80},{80,96},{96,112},{112,128},... | collective-permute-start | bytes 393224 | tf_op jit(solution)/shard_map/ppermute | solution.py:19
  93.0 42.1 %collective-permute-start.21 = (f32[4,128,64]{1,2,0:T(8,128)}, f32[4,128,64]{1,2,0:T(8,128)S(1)}, u32[]{:S(2)}, u32[]{:S(2)}) collective-permute-start(f32[4,128,64]{1,2,0:T(8,128)} %get-tuple-element.39), channel_id=1, source_target_pairs={{16,0},{32,16},{48,32},{64,48},{80,64},{96,80},{112,96},{128,112},... | collective-permute-start | bytes 393224 | tf_op jit(solution)/shard_map/ppermute | solution.py:22
  98.7 7.3 %collective-permute-start.6 = (f32[4,4,136]{1,2,0:T(8,128)S(1)}, f32[4,4,136]{1,2,0:T(8,128)S(1)}, u32[]{:S(2)}, u32[]{:S(2)}) collective-permute-start(f32[4,4,136]{1,2,0:T(8,128)S(1)} %get-tuple-element.36), channel_id=1, source_target_pairs={{0,1},{1,2},{2,3},{3,4},{4,5},{5,6},{6,7},{7,8},{8,9},{9,10},{10,1... | collective-permute-start | bytes 26120 | tf_op jit(solution)/shard_map/ppermute | solution.py:19
  101.6 9.9 %collective-permute-start.7 = (f32[4,4,136]{1,2,0:T(8,128)S(1)}, f32[4,4,136]{1,2,0:T(8,128)S(1)}, u32[]{:S(2)}, u32[]{:S(2)}) collective-permute-start(f32[4,4,136]{1,2,0:T(8,128)S(1)} %get-tuple-element.37), channel_id=1, source_target_pairs={{1,0},{2,1},{3,2},{4,3},{5,4},{6,5},{7,6},{8,7},{9,8},{10,9},{11,1... | collective-permute-start | bytes 26120 | tf_op jit(solution)/shard_map/ppermute | solution.py:22
  104.1 11.5 %collective-permute-start.12 = (f32[4,128,16]{1,2,0:T(8,128)}, f32[4,128,16]{1,2,0:T(8,128)S(1)}, u32[]{:S(2)}, u32[]{:S(2)}) collective-permute-start(f32[4,128,16]{1,2,0:T(8,128)} %get-tuple-element.40), channel_id=1, source_target_pairs={{0,16},{16,32},{32,48},{48,64},{64,80},{80,96},{96,112},{112,128},... | collective-permute-start | bytes 98312 | tf_op jit(solution)/shard_map/ppermute | solution.py:19
  106.0 9.6 %collective-permute-start.13 = (f32[4,128,16]{1,2,0:T(8,128)S(1)}, f32[4,128,16]{1,2,0:T(8,128)S(1)}, u32[]{:S(2)}, u32[]{:S(2)}) collective-permute-start(f32[4,128,16]{1,2,0:T(8,128)S(1)} %get-tuple-element.41), channel_id=1, source_target_pairs={{16,0},{32,16},{48,32},{64,48},{80,64},{96,80},{112,96},{128,112},... | collective-permute-start | bytes 98312 | tf_op jit(solution)/shard_map/ppermute | solution.py:22
  115.8 9.4 %collective-permute-start.14 = (f32[4,16,160]{1,2,0:T(8,128)S(1)}, f32[4,16,160]{1,2,0:T(8,128)S(1)}, u32[]{:S(2)}, u32[]{:S(2)}) collective-permute-start(f32[4,16,160]{1,2,0:T(8,128)S(1)} %get-tuple-element.20), channel_id=1, source_target_pairs={{0,1},{1,2},{2,3},{3,4},{4,5},{5,6},{6,7},{7,8},{8,9},{9,10},{10,1... | collective-permute-start | bytes 122888 | tf_op jit(solution)/shard_map/ppermute | solution.py:19
  121.2 9.6 %collective-permute-start.15 = (f32[4,16,160]{1,2,0:T(8,128)S(1)}, f32[4,16,160]{1,2,0:T(8,128)S(1)}, u32[]{:S(2)}, u32[]{:S(2)}) collective-permute-start(f32[4,16,160]{1,2,0:T(8,128)S(1)} %get-tuple-element.21), channel_id=1, source_target_pairs={{1,0},{2,1},{3,2},{4,3},{5,4},{6,5},{7,6},{8,7},{9,8},{10,9},{11,1... | collective-permute-start | bytes 122888 | tf_op jit(solution)/shard_map/ppermute | solution.py:22
  123.4 1.8 %copy-start.6 = (f32[4,128,2,128]{1,3,2,0:T(8,128)}, f32[4,128,2,128]{1,3,2,0:T(8,128)S(1)}, u32[]{:S(2)}) copy-start(f32[4,128,2,128]{1,3,2,0:T(8,128)S(1)} %copy.15) | copy-start | bytes 1572868
  135.8 8.0 %collective-permute-start.22 = (f32[4,64,256]{1,2,0:T(8,128)S(1)}, f32[4,64,256]{1,2,0:T(8,128)S(1)}, u32[]{:S(2)}, u32[]{:S(2)}) collective-permute-start(f32[4,64,256]{1,2,0:T(8,128)S(1)} %get-tuple-element.11), channel_id=1, source_target_pairs={{0,1},{1,2},{2,3},{3,4},{4,5},{5,6},{6,7},{7,8},{8,9},{9,10},{10,1... | collective-permute-start | bytes 786440 | tf_op jit(solution)/shard_map/ppermute | solution.py:19
  137.7 11.7 %collective-permute-start.23 = (f32[4,64,256]{1,2,0:T(8,128)S(1)}, f32[4,64,256]{1,2,0:T(8,128)S(1)}, u32[]{:S(2)}, u32[]{:S(2)}) collective-permute-start(f32[4,64,256]{1,2,0:T(8,128)S(1)} %get-tuple-element.12), channel_id=1, source_target_pairs={{1,0},{2,1},{3,2},{4,3},{5,4},{6,5},{7,6},{8,7},{9,8},{10,9},{11,1... | collective-permute-start | bytes 786440 | tf_op jit(solution)/shard_map/ppermute | solution.py:22
  140.4 9.0 %copy-start.11 = (f32[4,128,64]{1,2,0:T(8,128)S(1)}, f32[4,128,64]{1,2,0:T(8,128)}, u32[]{:S(2)}) copy-start(f32[4,128,64]{1,2,0:T(8,128)} %copy-done.10) | copy-start | bytes 393220
  140.4 9.0 %copy-start.13 = (f32[4,128,64]{1,2,0:T(8,128)S(1)}, f32[4,128,64]{1,2,0:T(8,128)}, u32[]{:S(2)}) copy-start(f32[4,128,64]{1,2,0:T(8,128)} %copy-done.12) | copy-start | bytes 393220
  140.6 3.2 %copy-start.4 = (f32[4,128,2,128]{1,3,2,0:T(8,128)}, f32[4,128,2,128]{1,3,2,0:T(8,128)S(1)}, u32[]{:S(2)}) copy-start(f32[4,128,2,128]{1,3,2,0:T(8,128)S(1)} %copy.23) | copy-start | bytes 1572868
  (7 other events, 6.8 us)
where the time goes:
time: 156 us; the launch traced here: 155 us
  starting transfers between devices  81.3 us (52%)
  waiting for transfers between devices  26.1 us (17%)
  other arithmetic  24.7 us (16%)
  local copies, waits for them, and re-layouts  21.3 us (14%)
    ppermute x12, starting transfers between devices, extended_2(): lax.ppermute(lax.slice_in_dim(block, 0, width, axis=dim), axis, backward)  44.6 us
    ppermute x12, starting transfers between devices, extended_2(): lax.ppermute(lax.slice_in_dim(block, block.shape[dim] - width, None, axis...  36.7 us
    ppermute x12, waiting for transfers between devices, extended_2(): lax.ppermute(lax.slice_in_dim(block, 0, width, axis=dim), axis, backward)  20.7 us
    another operation x56, local copies, waits for them, and re-layouts  14.8 us
    another operation x40, other arithmetic  14.2 us
    ppermute x12, waiting for transfers between devices, extended_2(): lax.ppermute(lax.slice_in_dim(block, block.shape[dim] - width, None, axis...  5.36 us
    concatenate x3, other arithmetic, local(): fields = jnp.concatenate([members, analysis[None]], axis=0)  4.21 us
    unnamed x30, local copies, waits for them, and re-layouts  3.21 us
  transfers between devices with their start and end apart: 24, of which 7 were waited for; matrix products, arithmetic and copies ran while one was open for 20% of the time, Pallas kernels for 0%

commit v1 on v0

v1 whole, which is shorter than its diff:
```python
import jax
import jax.numpy as jnp
from jax import lax
from jax.experimental import pallas as pl
from jax.experimental.pallas import tpu as pltpu
from jax.sharding import PartitionSpec as P

RADII = (64, 16, 4)
PAD = 64
T = 128
E = T + 2 * PAD
MESH = pl.DeviceIdType.MESH
F32 = jnp.float32
BF16 = jnp.bfloat16


def split(value, terms):
    parts = []
    for _ in range(terms - 1):
        head = value.astype(BF16)
        parts.append(head)
        value = value - head.astype(F32)
    parts.append(value.astype(BF16))
    return parts


def dot(a, b):
    return jnp.dot(a, b, preferred_element_type=F32)


def side_column(lane, odd):
    if odd:
        return jnp.where(lane < PAD, lane - PAD, lane + PAD)
    return jnp.where(lane < PAD, lane + T, lane - T)


def band(a, b, radius):
    return jnp.where(jnp.abs(a - b) <= radius, 1.0, 0.0).astype(BF16)


def slope(gap, soft):
    return gap * lax.rsqrt(gap * gap + soft)


def kernel(
    mem_hbm, ana_hbm, land_hbm, out_ref,
    mem, ana, land, ctr, lft, rgt, go_l, go_r,
    vm, vt, hm, ht, sig,
    own2, s_r, s_l, q_r, q_l, ud, in_l, in_r, k_l, k_r,
    in_sem, ss, rs,
):
    gx, gy = lax.axis_index("gx"), lax.axis_index("gy")
    last_x, last_y = lax.axis_size("gx") - 1, lax.axis_size("gy") - 1
    par = lax.rem(gy, 2)
    mate = gy + 1 - 2 * par
    outer = gy - 1 + 2 * par
    has_l, has_r = gx > 0, gx < last_x
    has_o = jnp.logical_and(outer >= 0, outer <= last_y)
    has_ol, has_or = jnp.logical_and(has_l, has_o), jnp.logical_and(has_r, has_o)
    always = None

    def when(cond, fn):
        if cond is None:
            fn()
        else:
            pl.when(cond)(fn)

    dev = {
        "l": (gx - 1, gy), "r": (gx + 1, gy), "m": (gx, mate), "o": (gx, outer),
        "ol": (gx - 1, outer), "or": (gx + 1, outer),
    }
    to = {"l": has_l, "r": has_r, "m": always, "o": has_o, "ol": has_ol, "or": has_or}
    come = {"l": has_r, "r": has_l, "m": always, "o": has_o, "ol": has_or, "or": has_ol}

    barrier = pltpu.get_barrier_semaphore()
    for name in dev:
        def hello(name=name):
            pl.semaphore_signal(barrier, inc=1, device_id=dev[name], device_id_type=MESH)
        when(to[name], hello)

    loads = [
        pltpu.make_async_copy(mem_hbm, mem, in_sem.at[0]),
        pltpu.make_async_copy(ana_hbm, ana, in_sem.at[1]),
        pltpu.make_async_copy(land_hbm, land, in_sem.at[2]),
    ]
    for load in loads:
        load.start()

    def rows64(start):
        return pl.ds(pl.multiple_of(start, PAD), PAD)

    inner_src, inner_dst = rows64(2 * PAD - PAD * par), rows64(3 * PAD * par)
    outer_src, outer_dst = rows64(PAD + PAD * par), rows64(3 * PAD - 3 * PAD * par)
    to_mate, to_outer = rows64(3 * PAD - 3 * PAD * par), rows64(3 * PAD * par)
    near_mate, near_outer = rows64(PAD - PAD * par), rows64(PAD * par)
    mates_near, outers_near = rows64(PAD * par), rows64(PAD - PAD * par)
    body = pl.ds(PAD, T)
    lane = lax.broadcasted_iota(jnp.int32, (T, T), 1)
    low = lane < PAD
    low2 = lax.broadcasted_iota(jnp.int32, (E, T), 1) < PAD

    count = [0]
    sent = []

    def send(name, src, dst, only=None):
        k = count[0]
        count[0] += 1
        copy = pltpu.make_async_remote_copy(
            src_ref=src, dst_ref=dst, send_sem=ss.at[k], recv_sem=rs.at[k],
            device_id=dev[name], device_id_type=MESH,
        )
        here, there = (to[name], come[name]) if only is None else (only, only)
        when(here, copy.start)
        sent.append((here, copy))
        return there, copy

    def arrived(item):
        when(item[0], item[1].wait_recv)

    def fill(cond, ref, rows=None):
        def zero():
            if rows is None:
                ref[...] = jnp.zeros(ref.shape, ref.dtype)
            else:
                ref[:, rows, :] = jnp.zeros((ref.shape[0], PAD, T), ref.dtype)
        pl.when(cond)(zero)

    loads[0].wait()
    loads[1].wait()
    for m in range(4):
        ctr[m, body] = mem[m] - ana[...]
    for p in range(2):
        even = ctr[2 * p, body]
        odd = pltpu.roll(ctr[2 * p + 1, body], PAD, 1)
        go_r[p] = jnp.where(low, odd, even)
        go_l[p] = jnp.where(low, even, odd)

    peers = sum(c.astype(jnp.int32) for c in (has_l, has_r, has_o, has_ol, has_or)) + 1
    pl.semaphore_wait(barrier, peers)

    mains = []
    for p in range(2):
        mains.append(send("l", go_l.at[p], rgt.at[p, body]))
        mains.append(send("r", go_r.at[p], lft.at[p, body]))
    to_o = send("o", ctr.at[:, outer_src], ctr.at[:, outer_dst])
    to_m = send("m", ctr.at[:, inner_src], ctr.at[:, inner_dst])
    corners = [
        send("ol", go_l.at[:, near_outer], rgt.at[:, outer_dst]),
        send("or", go_r.at[:, near_outer], lft.at[:, outer_dst]),
    ]

    no_l, no_r, no_o = jnp.logical_not(has_l), jnp.logical_not(has_r), jnp.logical_not(has_o)
    edge = to_outer
    fill(no_l, lft)
    fill(no_r, rgt)
    fill(jnp.logical_and(no_o, has_l), lft, edge)
    fill(jnp.logical_and(no_o, has_r), rgt, edge)
    fill(no_o, ctr, edge)
    fill(no_l, in_l)
    fill(no_r, in_r)
    fill(no_o, ud, near_outer)
    fill(jnp.logical_not(has_ol), k_l, near_outer)
    fill(jnp.logical_not(has_or), k_r, near_outer)
    k_l[:, near_mate, :] = jnp.zeros((2, PAD, T), F32)
    k_r[:, near_mate, :] = jnp.zeros((2, PAD, T), F32)

    def iota(shape, axis):
        return lax.broadcasted_iota(jnp.int32, shape, axis)

    for i, r in enumerate(RADII):
        vm[pl.ds(i * T, T), :] = band(iota((T, E), 0), iota((T, E), 1) - PAD, r)
        vt[i] = band(iota((E, T), 0) - PAD, iota((E, T), 1), r)
        for odd in range(2):
            hm[odd, i, pl.ds(0, T)] = band(iota((T, T), 0), iota((T, T), 1), r)
            hm[odd, i, pl.ds(T, T)] = band(side_column(iota((T, T), 0), odd), iota((T, T), 1), r)
            ht[odd, pl.ds(i * T, T), pl.ds(0, T)] = band(iota((T, T), 0), iota((T, T), 1), r)
            ht[odd, pl.ds(i * T, T), pl.ds(T, T)] = band(iota((T, T), 0), side_column(iota((T, T), 1), odd), r)

    arrived(to_m)
    arrived(to_o)
    v_own = []
    for p in range(2):
        wide = jnp.concatenate([ctr[2 * p], ctr[2 * p + 1]], axis=1)
        v_own.append(sum(dot(vm[...], part) for part in split(wide, 3)))

    forwards = []
    for p in range(2):
        arrived(mains[2 * p])
        arrived(mains[2 * p + 1])
        forwards.append(send("m", lft.at[p, inner_src], lft.at[p, inner_dst], has_l))
        forwards.append(send("m", rgt.at[p, inner_src], rgt.at[p, inner_dst], has_r))
    for item in corners + forwards:
        arrived(item)

    pooled = [[None] * 4 for _ in RADII]
    for p in range(2):
        a, b = lft[p], rgt[p]
        wide = jnp.concatenate([jnp.where(low2, b, a), jnp.where(low2, a, b)], axis=1)
        v_side = sum(dot(vm[...], part) for part in split(wide, 3))
        for odd in range(2):
            for i in range(3):
                rows, cols = slice(i * T, (i + 1) * T), slice(odd * T, (odd + 1) * T)
                both = jnp.concatenate([v_own[p][rows, cols], v_side[rows, cols]], axis=1)
                pooled[i][2 * p + odd] = sum(dot(part, hm[odd, i]) for part in split(both, 3))

    loads[2].wait()
    weight = land[...].astype(F32)
    for i, r in enumerate(RADII):
        soft = 0.01 * (2 * r + 1) ** 2
        one, two = weight * (1 / (4 * (2 * r + 1))), weight * (1 / (12 * (2 * r + 1)))
        q = pooled[i]
        spread = [None] * 4
        for j in range(4):
            for k in range(j + 1, 4):
                s = slope(q[j] - q[k], soft)
                spread[j] = s if spread[j] is None else spread[j] + s
                spread[k] = -s if spread[k] is None else spread[k] - s
        for j in range(4):
            value = one * slope(q[j], soft) - two * spread[j]
            for h, part in enumerate(split(value, 2)):
                sig[h, i, :, pl.ds(j * T, T)] = part

    second = []
    for p in range(2):
        frame = []
        tall = [
            sum(dot(vt[i], sig[h, i, :, pl.ds(2 * p * T, 2 * T)]) for h in range(2)) for i in range(3)
        ]
        for odd in range(2):
            cols = slice(odd * T, (odd + 1) * T)
            flat = jnp.concatenate([t[:, cols] for t in tall], axis=1)
            full = sum(dot(part, ht[odd]) for part in split(flat, 2))
            own2[2 * p + odd] = full[:, :T]
            frame.append(full[:, T:])
        s_r[p] = jnp.where(low2, frame[0], frame[1])
        s_l[p] = jnp.where(low2, frame[1], frame[0])
        give = [
            send("m", s_r.at[p, to_mate], q_r.at[p]),
            send("m", s_l.at[p, to_mate], q_l.at[p]),
        ]
        second.append(send("l", s_l.at[p, outer_src], in_r.at[p, near_outer]))
        second.append(send("r", s_r.at[p, outer_src], in_l.at[p, near_outer]))
        second.append(send("ol", s_l.at[p, to_outer], k_r.at[p, outers_near]))
        second.append(send("or", s_r.at[p, to_outer], k_l.at[p, outers_near]))
        both = pl.ds(2 * p, 2)
        second.append(send("m", own2.at[both, to_mate], ud.at[both, mates_near]))
        second.append(send("o", own2.at[both, to_outer], ud.at[both, outers_near]))
        for item in give:
            arrived(item)
        s_r[p, inner_src] = s_r[p, inner_src] + q_r[p]
        s_l[p, inner_src] = s_l[p, inner_src] + q_l[p]
        second.append(send("l", s_l.at[p, inner_src], in_r.at[p, near_mate]))
        second.append(send("r", s_r.at[p, inner_src], in_l.at[p, near_mate]))

    for item in second:
        arrived(item)
    for p in range(2):
        a, b = in_l[p] + k_l[p], in_r[p] + k_r[p]
        e, o = 2 * p, 2 * p + 1
        out_ref[e] = own2[e, body] + ud[e] + jnp.where(low, a, b)
        out_ref[o] = own2[o, body] + ud[o] + pltpu.roll(jnp.where(low, b, a), PAD, 1)
    for here, copy in sent:
        when(here, copy.wait_send)


def local(members, analysis, land_sea):
    vmem = pltpu.VMEM
    return pl.pallas_call(
        kernel,
        out_shape=jax.ShapeDtypeStruct((4, T, T), F32),
        in_specs=[pl.BlockSpec(memory_space=pl.ANY)] * 3,
        out_specs=pl.BlockSpec(memory_space=vmem),
        scratch_shapes=[
            vmem((4, T, T), F32), vmem((T, T), F32), vmem((T, T), jnp.int32),
            vmem((4, E, T), F32), vmem((2, E, T), F32), vmem((2, E, T), F32),
            vmem((2, T, T), F32), vmem((2, T, T), F32),
            vmem((3 * T, E), BF16), vmem((3, E, T), BF16),
            vmem((2, 3, E, T), BF16), vmem((2, 3 * T, E), BF16),
            vmem((2, 3, T, 4 * T), BF16),
            vmem((4, E, T), F32), vmem((2, E, T), F32), vmem((2, E, T), F32),
            vmem((2, PAD, T), F32), vmem((2, PAD, T), F32),
            vmem((4, T, T), F32),
            vmem((2, T, T), F32), vmem((2, T, T), F32), vmem((2, T, T), F32), vmem((2, T, T), F32),
            pltpu.SemaphoreType.DMA((3,)),
            pltpu.SemaphoreType.DMA((32,)), pltpu.SemaphoreType.DMA((32,)),
        ],
        compiler_params=pltpu.CompilerParams(
            collective_id=0, has_side_effects=True, vmem_limit_bytes=40 * 1024 * 1024
        ),
    )(members, analysis, land_sea)


def solution(mesh):
    return jax.shard_map(
        local,
        mesh=mesh,
        in_specs=(P(None, "gy", "gx"), P("gy", "gx"), P("gy", "gx")),
        out_specs=P(None, "gy", "gx"),
        check_vma=False,
    )
```

time: 156 us -> 27.8 us (0.18)
  starting transfers between devices: 81.3 us -> 0 us
  waiting for transfers between devices: 26.1 us -> 0 us
  other arithmetic: 24.7 us -> 0 us
  Pallas kernels: 0 us -> 24 us
  local copies, waits for them, and re-layouts: 21.3 us -> 3.33 us
    ppermute x24 -> x0, starting transfers between devices: 81.3 us -> none  [the longest x12 44.6 us: extended_2(): lax.ppermute(lax.slice_in_dim(block, 0, width, axis=dim), axis, backward)]
    ppermute x24 -> x0, waiting for transfers between devices: 26.1 us -> none  [the longest x12 20.7 us: extended_2(): lax.ppermute(lax.slice_in_dim(block, 0, width, axis=dim), axis, backward)]
    pallas_call x0 -> x1, Pallas kernels: none -> 24 us  [local(): pl.pallas_call(kernel, out_shape=jax.ShapeDtypeStruct((4, T, T), F32), in...]
    another operation x56 -> x0, local copies, waits for them, and re-layouts: 14.8 us -> none
    another operation x40 -> x0, other arithmetic: 14.2 us -> none
    concatenate x8 -> x0, other arithmetic: 7.09 us -> none  [the longest x3 4.21 us: local(): fields = jnp.concatenate([members, analysis[None]], axis=0)]
    slice x7 -> x0, local copies, waits for them, and re-layouts: 1.88 us -> none  [extended_2(): lax.slice_in_dim(block, block.shape[dim] - width, None, axis=dim)]
    unnamed x30 -> x7, local copies, waits for them, and re-layouts: 3.21 us -> 3.33 us
  transfers between devices with their start and end apart: 24 -> 0, of which waited for: 7 -> 0; matrix products, arithmetic and copies ran while one was open for 20% -> 0% of each run, Pallas kernels for 0% -> 0%
where the time goes in v1:
time: 27.8 us; the launch traced here: 27.4 us
  Pallas kernels  24 us (86%)
  local copies, waits for them, and re-layouts  3.33 us (12%)
    pallas_call x1, Pallas kernels, local(): pl.pallas_call(kernel, out_shape=jax.ShapeDtypeStruct((4, T, T), F32), in...  24 us
    unnamed x7, local copies, waits for them, and re-layouts  3.33 us

profile of v1, /device:TPU:99, one launch (start us, length us, event | category | flops | bytes accessed | tf_op | source)
XLA Modules:
  0.0 27.4 jit_solution(9978899529315725343)
XLA Ops:
  0.0 0.0 copy-start
  0.0 0.9 %copy-done = f32[4,128,128]{2,1,0:T(8,128)S(1)} copy-done((f32[4,128,128]{2,1,0:T(8,128)S(1)}, f32[4,128,128]{2,1,0:T(8,128)}, u32[]{:S(2)}) %copy-start) | copy-done | bytes 262168
  1.0 0.0 copy-start.1
  1.0 0.8 %copy-done.1 = f32[128,128]{1,0:T(8,128)S(1)} copy-done((f32[128,128]{1,0:T(8,128)S(1)}, f32[128,128]{1,0:T(8,128)}, u32[]{:S(2)}) %copy-start.1) | copy-done | bytes 65560
  1.8 0.0 copy-start.2
  1.8 0.8 %copy-done.2 = s32[128,128]{1,0:T(8,128)S(1)} copy-done((s32[128,128]{1,0:T(8,128)S(1)}, s32[128,128]{1,0:T(8,128)}, u32[]{:S(2)}) %copy-start.2) | copy-done | bytes 65560
  2.6 24.0 %shard_map.37 = f32[4,128,128]{2,1,0:T(8,128)S(1)} custom-call(f32[4,128,128]{2,1,0:T(8,128)S(1)} %copy-done, f32[128,128]{1,0:T(8,128)S(1)} %copy-done.1, s32[128,128]{1,0:T(8,128)S(1)} %copy-done.2), custom_call_target="tpu_custom_call" | custom-call | tf_op jit(solution)/shard_map/pallas_call | solution.py:268
  26.7 0.7 %copy.5 = f32[4,128,128]{2,1,0:T(8,128)} copy(f32[4,128,128]{2,1,0:T(8,128)S(1)} %shard_map.37) | data formatting | bytes 524288
Async XLA Ops:
  0.0 0.9 %copy-start = (f32[4,128,128]{2,1,0:T(8,128)S(1)}, f32[4,128,128]{2,1,0:T(8,128)}, u32[]{:S(2)}) copy-start(f32[4,128,128]{2,1,0:T(8,128)} %mem_hbm.1) | copy-start | bytes 786436
  1.0 0.8 %copy-start.1 = (f32[128,128]{1,0:T(8,128)S(1)}, f32[128,128]{1,0:T(8,128)}, u32[]{:S(2)}) copy-start(f32[128,128]{1,0:T(8,128)} %ana_hbm.1) | copy-start | bytes 196612
  1.8 0.8 %copy-start.2 = (s32[128,128]{1,0:T(8,128)S(1)}, s32[128,128]{1,0:T(8,128)}, u32[]{:S(2)}) copy-start(s32[128,128]{1,0:T(8,128)} %land_hbm.1) | copy-start | bytes 196612

commit v2 on v1

--- a/solution.py
+++ b/solution.py
@@ -287,7 +287,7 @@
         compiler_params=pltpu.CompilerParams(
             collective_id=0, has_side_effects=True, vmem_limit_bytes=40 * 1024 * 1024
         ),
-    )(members, analysis, land_sea)
+    )(*(pltpu.with_memory_space_constraint(x, pltpu.HBM) for x in (members, analysis, land_sea)))
 
 
 def solution(mesh):

time: 27.8 us -> 25.1 us (0.903)
  local copies, waits for them, and re-layouts: 3.33 us -> 0.71 us
    unnamed x7 -> x1, local copies, waits for them, and re-layouts: 3.33 us -> 0.71 us
where the time goes in v2:
time: 25.1 us; the launch traced here: 24.7 us
  Pallas kernels  24 us (96%)
  local copies, waits for them, and re-layouts  0.71 us (3%)
    pallas_call x1, Pallas kernels, local(): pl.pallas_call(kernel, out_shape=jax.ShapeDtypeStruct((4, T, T), F32), in...  24 us
    unnamed x1, local copies, waits for them, and re-layouts  0.71 us

profile of v2, /device:TPU:99, one launch (start us, length us, event | category | flops | bytes accessed | tf_op | source)
XLA Modules:
  0.0 24.7 jit_solution(6809861639880131213)
XLA Ops:
  0.0 24.0 %shard_map.37 = f32[4,128,128]{2,1,0:T(8,128)S(1)} custom-call(f32[4,128,128]{2,1,0:T(8,128)} %mem_hbm.1, f32[128,128]{1,0:T(8,128)} %ana_hbm.1, s32[128,128]{1,0:T(8,128)} %land_hbm.1), custom_call_target="tpu_custom_call" | custom-call | tf_op jit(solution)/shard_map/pallas_call | solution.py:268
  24.0 0.7 %copy.5 = f32[4,128,128]{2,1,0:T(8,128)} copy(f32[4,128,128]{2,1,0:T(8,128)S(1)} %shard_map.37) | data formatting | bytes 524288

commit v3 on v2

--- a/solution.py
+++ b/solution.py
@@ -42,12 +42,17 @@
     return gap * lax.rsqrt(gap * gap + soft)
 
 
+NEAR = 16
+FAR = PAD - NEAR
+MID = T + 2 * NEAR
+
+
 def kernel(
     mem_hbm, ana_hbm, land_hbm, out_ref,
     mem, ana, land, ctr, lft, rgt, go_l, go_r,
-    vm, vt, hm, ht, sig,
+    vm, vs, vt, hm, ht, sig, base,
     own2, s_r, s_l, q_r, q_l, ud, in_l, in_r, k_l, k_r,
-    in_sem, ss, rs,
+    in_sem, ss, rs, ok,
 ):
     gx, gy = lax.axis_index("gx"), lax.axis_index("gy")
     last_x, last_y = lax.axis_size("gx") - 1, lax.axis_size("gy") - 1
@@ -72,11 +77,14 @@
     to = {"l": has_l, "r": has_r, "m": always, "o": has_o, "ol": has_ol, "or": has_or}
     come = {"l": has_r, "r": has_l, "m": always, "o": has_o, "ol": has_or, "or": has_ol}
 
+    def tell(semaphore, name, cond):
+        def signal():
+            pl.semaphore_signal(semaphore, inc=1, device_id=dev[name], device_id_type=MESH)
+        when(cond, signal)
+
     barrier = pltpu.get_barrier_semaphore()
-    for name in dev:
-        def hello(name=name):
-            pl.semaphore_signal(barrier, inc=1, device_id=dev[name], device_id_type=MESH)
-        when(to[name], hello)
+    for name in ("l", "r", "o", "m"):
+        tell(barrier, name, to[name])
 
     loads = [
         pltpu.make_async_copy(mem_hbm, mem, in_sem.at[0]),
@@ -86,18 +94,25 @@
     for load in loads:
         load.start()
 
-    def rows64(start):
-        return pl.ds(pl.multiple_of(start, PAD), PAD)
-
-    inner_src, inner_dst = rows64(2 * PAD - PAD * par), rows64(3 * PAD * par)
-    outer_src, outer_dst = rows64(PAD + PAD * par), rows64(3 * PAD - 3 * PAD * par)
-    to_mate, to_outer = rows64(3 * PAD - 3 * PAD * par), rows64(3 * PAD * par)
-    near_mate, near_outer = rows64(PAD - PAD * par), rows64(PAD * par)
-    mates_near, outers_near = rows64(PAD * par), rows64(PAD - PAD * par)
-    body = pl.ds(PAD, T)
-    lane = lax.broadcasted_iota(jnp.int32, (T, T), 1)
-    low = lane < PAD
-    low2 = lax.broadcasted_iota(jnp.int32, (E, T), 1) < PAD
+    def rows(start, size=PAD):
+        return pl.ds(pl.multiple_of(start, NEAR), size)
+
+    inner_src, inner_dst = rows(2 * PAD - PAD * par), rows(3 * PAD * par)
+    outer_src, outer_dst = rows(PAD + PAD * par), rows(3 * PAD - 3 * PAD * par)
+    to_mate, to_outer = rows(3 * PAD - 3 * PAD * par), rows(3 * PAD * par)
+    outer_half, inner_half = rows(T * par, T), rows(T - T * par, T)
+    near_mate, near_outer = rows(PAD - PAD * par), rows(PAD * par)
+    mates_near, outers_near = rows(PAD * par), rows(PAD - PAD * par)
+    edge_src, edge_dst = rows((T - NEAR) * par, NEAR), rows(3 * PAD - (2 * PAD + NEAR) * par, NEAR)
+    far_src, far_dst = rows(NEAR + FAR * par, FAR), rows((3 * PAD + NEAR) * (1 - par), FAR)
+    body, middle = pl.ds(PAD, T), pl.ds(PAD - NEAR, MID)
+
+    def iota(shape, axis):
+        return lax.broadcasted_iota(jnp.int32, shape, axis)
+
+    low = iota((T, T), 1) < PAD
+    low_mid = iota((MID, T), 1) < PAD
+    low_all = iota((E, T), 1) < PAD
 
     count = [0]
     sent = []
@@ -117,12 +132,12 @@
     def arrived(item):
         when(item[0], item[1].wait_recv)
 
-    def fill(cond, ref, rows=None):
+    def fill(cond, ref, part=None):
         def zero():
-            if rows is None:
+            if part is None:
                 ref[...] = jnp.zeros(ref.shape, ref.dtype)
             else:
-                ref[:, rows, :] = jnp.zeros((ref.shape[0], PAD, T), ref.dtype)
+                ref[:, part, :] = jnp.zeros((ref.shape[0], PAD, T), ref.dtype)
         pl.when(cond)(zero)
 
     loads[0].wait()
@@ -135,27 +150,24 @@
         go_r[p] = jnp.where(low, odd, even)
         go_l[p] = jnp.where(low, even, odd)
 
-    peers = sum(c.astype(jnp.int32) for c in (has_l, has_r, has_o, has_ol, has_or)) + 1
+    peers = sum(c.astype(jnp.int32) for c in (has_l, has_r, has_o)) + 1
     pl.semaphore_wait(barrier, peers)
 
+    tell(ok.at[1], "l", has_ol)
+    tell(ok.at[0], "r", has_or)
     mains = []
     for p in range(2):
         mains.append(send("l", go_l.at[p], rgt.at[p, body]))
         mains.append(send("r", go_r.at[p], lft.at[p, body]))
     to_o = send("o", ctr.at[:, outer_src], ctr.at[:, outer_dst])
     to_m = send("m", ctr.at[:, inner_src], ctr.at[:, inner_dst])
-    corners = [
-        send("ol", go_l.at[:, near_outer], rgt.at[:, outer_dst]),
-        send("or", go_r.at[:, near_outer], lft.at[:, outer_dst]),
-    ]
 
     no_l, no_r, no_o = jnp.logical_not(has_l), jnp.logical_not(has_r), jnp.logical_not(has_o)
-    edge = to_outer
     fill(no_l, lft)
     fill(no_r, rgt)
-    fill(jnp.logical_and(no_o, has_l), lft, edge)
-    fill(jnp.logical_and(no_o, has_r), rgt, edge)
-    fill(no_o, ctr, edge)
+    fill(jnp.logical_and(no_o, has_l), lft, to_outer)
+    fill(jnp.logical_and(no_o, has_r), rgt, to_outer)
+    fill(no_o, ctr, to_outer)
     fill(no_l, in_l)
     fill(no_r, in_r)
     fill(no_o, ud, near_outer)
@@ -164,11 +176,23 @@
     k_l[:, near_mate, :] = jnp.zeros((2, PAD, T), F32)
     k_r[:, near_mate, :] = jnp.zeros((2, PAD, T), F32)
 
-    def iota(shape, axis):
-        return lax.broadcasted_iota(jnp.int32, shape, axis)
-
     for i, r in enumerate(RADII):
         vm[pl.ds(i * T, T), :] = band(iota((T, E), 0), iota((T, E), 1) - PAD, r)
+        if i:
+            vs[pl.ds((i - 1) * T, T), :] = band(iota((T, MID), 0), iota((T, MID), 1) - NEAR, r)
+
+    when(has_ol, lambda: pl.semaphore_wait(ok.at[0], 1))
+    when(has_or, lambda: pl.semaphore_wait(ok.at[1], 1))
+    edges = [
+        send("ol", go_l.at[:, edge_src], rgt.at[:, edge_dst]),
+        send("or", go_r.at[:, edge_src], lft.at[:, edge_dst]),
+    ]
+    fars = [
+        send("ol", go_l.at[:, far_src], rgt.at[:, far_dst]),
+        send("or", go_r.at[:, far_src], lft.at[:, far_dst]),
+    ]
+
+    for i, r in enumerate(RADII):
         vt[i] = band(iota((E, T), 0) - PAD, iota((E, T), 1), r)
         for odd in range(2):
             hm[odd, i, pl.ds(0, T)] = band(iota((T, T), 0), iota((T, T), 1), r)
@@ -189,26 +213,23 @@
         arrived(mains[2 * p + 1])
         forwards.append(send("m", lft.at[p, inner_src], lft.at[p, inner_dst], has_l))
         forwards.append(send("m", rgt.at[p, inner_src], rgt.at[p, inner_dst], has_r))
-    for item in corners + forwards:
-        arrived(item)
-
-    pooled = [[None] * 4 for _ in RADII]
-    for p in range(2):
-        a, b = lft[p], rgt[p]
-        wide = jnp.concatenate([jnp.where(low2, b, a), jnp.where(low2, a, b)], axis=1)
-        v_side = sum(dot(vm[...], part) for part in split(wide, 3))
-        for odd in range(2):
-            for i in range(3):
-                rows, cols = slice(i * T, (i + 1) * T), slice(odd * T, (odd + 1) * T)
-                both = jnp.concatenate([v_own[p][rows, cols], v_side[rows, cols]], axis=1)
-                pooled[i][2 * p + odd] = sum(dot(part, hm[odd, i]) for part in split(both, 3))
 
     loads[2].wait()
     weight = land[...].astype(F32)
-    for i, r in enumerate(RADII):
+
+    def side(p, part, mask):
+        a, b = lft[p, part], rgt[p, part]
+        return jnp.concatenate([jnp.where(mask, b, a), jnp.where(mask, a, b)], axis=1)
+
+    def pooled(i, p, odd, v_side):
+        cols = slice(odd * T, (odd + 1) * T)
+        both = jnp.concatenate([v_own[p][i * T : (i + 1) * T, cols], v_side[:, cols]], axis=1)
+        return sum(dot(part, hm[odd, i]) for part in split(both, 3))
+
+    def slopes(i, q):
+        r = RADII[i]
         soft = 0.01 * (2 * r + 1) ** 2
         one, two = weight * (1 / (4 * (2 * r + 1))), weight * (1 / (12 * (2 * r + 1)))
-        q = pooled[i]
         spread = [None] * 4
         for j in range(4):
             for k in range(j + 1, 4):
@@ -220,33 +241,62 @@
             for h, part in enumerate(split(value, 2)):
                 sig[h, i, :, pl.ds(j * T, T)] = part
 
-    second = []
-    for p in range(2):
-        frame = []
-        tall = [
-            sum(dot(vt[i], sig[h, i, :, pl.ds(2 * p * T, 2 * T)]) for h in range(2)) for i in range(3)
-        ]
+    def tall(i, p, part):
+        return sum(dot(vt[i, part], sig[h, i, :, pl.ds(2 * p * T, 2 * T)]) for h in range(2))
+
+    for item in edges + forwards:
+        arrived(item)
+    small = []
+    for p in range(2):
+        small.append(sum(dot(vs[...], part) for part in split(side(p, middle, low_mid), 3)))
+    for i in (1, 2):
+        slopes(i, [pooled(i, m // 2, m % 2, small[m // 2][(i - 1) * T : i * T]) for m in range(4)])
+    for p in range(2):
+        both = [tall(i, p, pl.ds(0, E)) for i in (1, 2)]
         for odd in range(2):
             cols = slice(odd * T, (odd + 1) * T)
-            flat = jnp.concatenate([t[:, cols] for t in tall], axis=1)
-            full = sum(dot(part, ht[odd]) for part in split(flat, 2))
-            own2[2 * p + odd] = full[:, :T]
+            flat = jnp.concatenate([t[:, cols] for t in both], axis=1)
+            base[2 * p + odd] = sum(dot(part, ht[odd, pl.ds(T, 2 * T)]) for part in split(flat, 2))
+
+    for item in fars:
+        arrived(item)
+    q = []
+    for p in range(2):
+        v_side = sum(dot(vm[pl.ds(0, T)], part) for part in split(side(p, pl.ds(0, E), low_all), 3))
+        q += [pooled(0, p, odd, v_side) for odd in range(2)]
+    slopes(0, q)
+
+    def piece(p, half):
+        high = tall(0, p, half)
+        frame = []
+        for odd in range(2):
+            cols = slice(odd * T, (odd + 1) * T)
+            full = base[2 * p + odd, half] + sum(
+                dot(part, ht[odd, pl.ds(0, T)]) for part in split(high[:, cols], 2)
+            )
+            own2[2 * p + odd, half] = full[:, :T]
             frame.append(full[:, T:])
-        s_r[p] = jnp.where(low2, frame[0], frame[1])
-        s_l[p] = jnp.where(low2, frame[1], frame[0])
-        give = [
-            send("m", s_r.at[p, to_mate], q_r.at[p]),
-            send("m", s_l.at[p, to_mate], q_l.at[p]),
-        ]
+        s_r[p, half] = jnp.where(low, frame[0], frame[1])
+        s_l[p, half] = jnp.where(low, frame[1], frame[0])
+
+    second, give = [], []
+    for p in range(2):
+        piece(p, outer_half)
+        both = pl.ds(2 * p, 2)
+        second.append(send("ol", s_l.at[p, to_outer], k_r.at[p, outers_near]))
+        second.append(send("or", s_r.at[p, to_outer], k_l.at[p, outers_near]))
         second.append(send("l", s_l.at[p, outer_src], in_r.at[p, near_outer]))
         second.append(send("r", s_r.at[p, outer_src], in_l.at[p, near_outer]))
-        second.append(send("ol", s_l.at[p, to_outer], k_r.at[p, outers_near]))
-        second.append(send("or", s_r.at[p, to_outer], k_l.at[p, outers_near]))
+        second.append(send("o", own2.at[both, to_outer], ud.at[both, outers_near]))
+    for p in range(2):
+        piece(p, inner_half)
         both = pl.ds(2 * p, 2)
+        give.append(send("m", s_r.at[p, to_mate], q_r.at[p]))
+        give.append(send("m", s_l.at[p, to_mate], q_l.at[p]))
         second.append(send("m", own2.at[both, to_mate], ud.at[both, mates_near]))
-        second.append(send("o", own2.at[both, to_outer], ud.at[both, outers_near]))
-        for item in give:
-            arrived(item)
+    for p in range(2):
+        arrived(give[2 * p])
+        arrived(give[2 * p + 1])
         s_r[p, inner_src] = s_r[p, inner_src] + q_r[p]
         s_l[p, inner_src] = s_l[p, inner_src] + q_l[p]
         second.append(send("l", s_l.at[p, inner_src], in_r.at[p, near_mate]))
@@ -274,15 +324,16 @@
             vmem((4, T, T), F32), vmem((T, T), F32), vmem((T, T), jnp.int32),
             vmem((4, E, T), F32), vmem((2, E, T), F32), vmem((2, E, T), F32),
             vmem((2, T, T), F32), vmem((2, T, T), F32),
-            vmem((3 * T, E), BF16), vmem((3, E, T), BF16),
+            vmem((3 * T, E), BF16), vmem((2 * T, MID), BF16), vmem((3, E, T), BF16),
             vmem((2, 3, E, T), BF16), vmem((2, 3 * T, E), BF16),
-            vmem((2, 3, T, 4 * T), BF16),
+            vmem((2, 3, T, 4 * T), BF16), vmem((4, E, E), F32),
             vmem((4, E, T), F32), vmem((2, E, T), F32), vmem((2, E, T), F32),
             vmem((2, PAD, T), F32), vmem((2, PAD, T), F32),
             vmem((4, T, T), F32),
             vmem((2, T, T), F32), vmem((2, T, T), F32), vmem((2, T, T), F32), vmem((2, T, T), F32),
             pltpu.SemaphoreType.DMA((3,)),
-            pltpu.SemaphoreType.DMA((32,)), pltpu.SemaphoreType.DMA((32,)),
+            pltpu.SemaphoreType.DMA((40,)), pltpu.SemaphoreType.DMA((40,)),
+            pltpu.SemaphoreType.REGULAR((2,)),
         ],
         compiler_params=pltpu.CompilerParams(
             collective_id=0, has_side_effects=True, vmem_limit_bytes=40 * 1024 * 1024

time: 25.1 us -> 22.9 us (0.912)
  Pallas kernels: 24 us -> 21.9 us
    pallas_call x1, Pallas kernels: 24 us -> 21.9 us  [local(): pl.pallas_call(kernel, out_shape=jax.ShapeDtypeStruct((4, T, T), F32), in...]
where the time goes in v3:
time: 22.9 us; the launch traced here: 22.7 us
  Pallas kernels  21.9 us (96%)
  local copies, waits for them, and re-layouts  0.71 us (3%)
    pallas_call x1, Pallas kernels, local(): pl.pallas_call(kernel, out_shape=jax.ShapeDtypeStruct((4, T, T), F32), in...  21.9 us
    unnamed x1, local copies, waits for them, and re-layouts  0.71 us

profile of v3, /device:TPU:99, one launch (start us, length us, event | category | flops | bytes accessed | tf_op | source)
XLA Modules:
  0.0 22.7 jit_solution(13490029168980853772)
XLA Ops:
  0.0 21.9 %shard_map.37 = f32[4,128,128]{2,1,0:T(8,128)S(1)} custom-call(f32[4,128,128]{2,1,0:T(8,128)} %mem_hbm.1, f32[128,128]{1,0:T(8,128)} %ana_hbm.1, s32[128,128]{1,0:T(8,128)} %land_hbm.1), custom_call_target="tpu_custom_call" | custom-call | tf_op jit(solution)/shard_map/pallas_call | solution.py:318
  22.0 0.7 %copy.5 = f32[4,128,128]{2,1,0:T(8,128)} copy(f32[4,128,128]{2,1,0:T(8,128)S(1)} %shard_map.37) | data formatting | bytes 524288

commit v4 on v3

--- a/solution.py
+++ b/solution.py
@@ -43,14 +43,14 @@
 
 
 NEAR = 16
-FAR = PAD - NEAR
-MID = T + 2 * NEAR
+REST = E - PAD
+LATE = PAD + 2 * NEAR
 
 
 def kernel(
     mem_hbm, ana_hbm, land_hbm, out_ref,
     mem, ana, land, ctr, lft, rgt, go_l, go_r,
-    vm, vs, vt, hm, ht, sig, base,
+    vm, ve, vl, vt, hm, ht, sig, qs,
     own2, s_r, s_l, q_r, q_l, ud, in_l, in_r, k_l, k_r,
     in_sem, ss, rs, ok,
 ):
@@ -103,16 +103,19 @@
     outer_half, inner_half = rows(T * par, T), rows(T - T * par, T)
     near_mate, near_outer = rows(PAD - PAD * par), rows(PAD * par)
     mates_near, outers_near = rows(PAD * par), rows(PAD - PAD * par)
-    edge_src, edge_dst = rows((T - NEAR) * par, NEAR), rows(3 * PAD - (2 * PAD + NEAR) * par, NEAR)
-    far_src, far_dst = rows(NEAR + FAR * par, FAR), rows((3 * PAD + NEAR) * (1 - par), FAR)
-    body, middle = pl.ds(PAD, T), pl.ds(PAD - NEAR, MID)
+    rest = rows(PAD - PAD * par, REST)
+    touched = (PAD * par, (T - NEAR) * par, (T - NEAR) * par)
+    apart = (PAD - PAD * par, NEAR - NEAR * par, NEAR - NEAR * par)
+    sizes = (PAD, NEAR, NEAR)
+    begins = (0, PAD, PAD + NEAR)
+    body = pl.ds(PAD, T)
 
     def iota(shape, axis):
         return lax.broadcasted_iota(jnp.int32, shape, axis)
 
     low = iota((T, T), 1) < PAD
-    low_mid = iota((MID, T), 1) < PAD
-    low_all = iota((E, T), 1) < PAD
+    low_rest = iota((REST, T), 1) < PAD
+    low_pad = iota((PAD, T), 1) < PAD
 
     count = [0]
     sent = []
@@ -153,8 +156,7 @@
     peers = sum(c.astype(jnp.int32) for c in (has_l, has_r, has_o)) + 1
     pl.semaphore_wait(barrier, peers)
 
-    tell(ok.at[1], "l", has_ol)
-    tell(ok.at[0], "r", has_or)
+    tell(ok, "o", has_o)
     mains = []
     for p in range(2):
         mains.append(send("l", go_l.at[p], rgt.at[p, body]))
@@ -177,35 +179,45 @@
     k_r[:, near_mate, :] = jnp.zeros((2, PAD, T), F32)
 
     for i, r in enumerate(RADII):
-        vm[pl.ds(i * T, T), :] = band(iota((T, E), 0), iota((T, E), 1) - PAD, r)
-        if i:
-            vs[pl.ds((i - 1) * T, T), :] = band(iota((T, MID), 0), iota((T, MID), 1) - NEAR, r)
-
-    when(has_ol, lambda: pl.semaphore_wait(ok.at[0], 1))
-    when(has_or, lambda: pl.semaphore_wait(ok.at[1], 1))
-    edges = [
-        send("ol", go_l.at[:, edge_src], rgt.at[:, edge_dst]),
-        send("or", go_r.at[:, edge_src], lft.at[:, edge_dst]),
+        whole = band(iota((T, E), 0), iota((T, E), 1) - PAD, r)
+        most = band(iota((T, REST), 0), iota((T, REST), 1) - PAD * par, r)
+        first = (PAD, T - NEAR, T - NEAR)[i] * par
+        few = band(iota((sizes[i], PAD), 0) + first, iota((sizes[i], PAD), 1) - PAD + 3 * PAD * par, r)
+        vm[pl.ds(i * T, T), :] = jnp.concatenate([whole] * 3, axis=1)
+        ve[pl.ds(i * T, T), :] = jnp.concatenate([most] * 3, axis=1)
+        vl[pl.ds(begins[i], sizes[i]), :] = jnp.concatenate([few] * 3, axis=1)
+
+    when(has_o, lambda: pl.semaphore_wait(ok, 1))
+    corners = [
+        send("ol", go_l.at[:, near_outer], rgt.at[:, outer_dst]),
+        send("or", go_r.at[:, near_outer], lft.at[:, outer_dst]),
     ]
-    fars = [
-        send("ol", go_l.at[:, far_src], rgt.at[:, far_dst]),
-        send("or", go_r.at[:, far_src], lft.at[:, far_dst]),
-    ]
-
+
+    nought = jnp.zeros((T, T), BF16)
     for i, r in enumerate(RADII):
-        vt[i] = band(iota((E, T), 0) - PAD, iota((E, T), 1), r)
+        square = band(iota((T, T), 0), iota((T, T), 1), r)
+        sides = [band(side_column(iota((T, T), 0), odd), iota((T, T), 1), r) for odd in range(2)]
+        back = [band(iota((T, T), 0), side_column(iota((T, T), 1), odd), r) for odd in range(2)]
+        for first, blocks in ((0, [square, square]), (1, sides)):
+            hm[first, i, pl.ds(0, T)] = jnp.concatenate([blocks[0], nought], axis=1)
+            hm[first, i, pl.ds(T, T)] = jnp.concatenate([nought, blocks[1]], axis=1)
+        vt[i] = jnp.concatenate([band(iota((E, T), 0) - PAD, iota((E, T), 1), r)] * 2, axis=1)
         for odd in range(2):
-            hm[odd, i, pl.ds(0, T)] = band(iota((T, T), 0), iota((T, T), 1), r)
-            hm[odd, i, pl.ds(T, T)] = band(side_column(iota((T, T), 0), odd), iota((T, T), 1), r)
-            ht[odd, pl.ds(i * T, T), pl.ds(0, T)] = band(iota((T, T), 0), iota((T, T), 1), r)
-            ht[odd, pl.ds(i * T, T), pl.ds(T, T)] = band(iota((T, T), 0), side_column(iota((T, T), 1), odd), r)
+            for h in range(2):
+                ht[odd, pl.ds((3 * h + i) * T, T)] = jnp.concatenate([square, back[odd]], axis=1)
+
+    def along_rows(pair, first, i):
+        size = pair.shape[0]
+        out = dot(jnp.concatenate(split(pair, 3), axis=0), hm[first, i])
+        return out[:size] + out[size : 2 * size] + out[2 * size :]
 
     arrived(to_m)
     arrived(to_o)
-    v_own = []
     for p in range(2):
         wide = jnp.concatenate([ctr[2 * p], ctr[2 * p + 1]], axis=1)
-        v_own.append(sum(dot(vm[...], part) for part in split(wide, 3)))
+        v_own = dot(vm[...], jnp.concatenate(split(wide, 3), axis=0))
+        for i in range(3):
+            qs[i, p] = along_rows(v_own[i * T : (i + 1) * T], 0, i)
 
     forwards = []
     for p in range(2):
@@ -215,19 +227,15 @@
         forwards.append(send("m", rgt.at[p, inner_src], rgt.at[p, inner_dst], has_r))
 
     loads[2].wait()
-    weight = land[...].astype(F32)
 
     def side(p, part, mask):
         a, b = lft[p, part], rgt[p, part]
         return jnp.concatenate([jnp.where(mask, b, a), jnp.where(mask, a, b)], axis=1)
 
-    def pooled(i, p, odd, v_side):
-        cols = slice(odd * T, (odd + 1) * T)
-        both = jnp.concatenate([v_own[p][i * T : (i + 1) * T, cols], v_side[:, cols]], axis=1)
-        return sum(dot(part, hm[odd, i]) for part in split(both, 3))
-
-    def slopes(i, q):
-        r = RADII[i]
+    def slopes(i, start, q):
+        r, size = RADII[i], q[0].shape[0]
+        q = [pair[:, odd * T : (odd + 1) * T] for pair in q for odd in range(2)]
+        weight = land[rows(start, size)].astype(F32)
         soft = 0.01 * (2 * r + 1) ** 2
         one, two = weight * (1 / (4 * (2 * r + 1))), weight * (1 / (12 * (2 * r + 1)))
         spread = [None] * 4
@@ -238,42 +246,35 @@
                 spread[k] = -s if spread[k] is None else spread[k] - s
         for j in range(4):
             value = one * slope(q[j], soft) - two * spread[j]
-            for h, part in enumerate(split(value, 2)):
-                sig[h, i, :, pl.ds(j * T, T)] = part
-
-    def tall(i, p, part):
-        return sum(dot(vt[i, part], sig[h, i, :, pl.ds(2 * p * T, 2 * T)]) for h in range(2))
-
-    for item in edges + forwards:
+            for h, piece in enumerate(split(value, 2)):
+                sig[i, rows(h * T + start, size), pl.ds(j * T, T)] = piece
+
+    for p in range(2):
+        arrived(forwards[2 * p])
+        arrived(forwards[2 * p + 1])
+        v_side = dot(ve[...], jnp.concatenate(split(side(p, rest, low_rest), 3), axis=0))
+        for i in range(3):
+            qs[i, p] = qs[i, p] + along_rows(v_side[i * T : (i + 1) * T], 1, i)
+    for i in range(3):
+        slopes(i, apart[i], [qs[i, p, rows(apart[i], T - sizes[i])] for p in range(2)])
+
+    for item in corners:
         arrived(item)
-    small = []
-    for p in range(2):
-        small.append(sum(dot(vs[...], part) for part in split(side(p, middle, low_mid), 3)))
-    for i in (1, 2):
-        slopes(i, [pooled(i, m // 2, m % 2, small[m // 2][(i - 1) * T : i * T]) for m in range(4)])
-    for p in range(2):
-        both = [tall(i, p, pl.ds(0, E)) for i in (1, 2)]
-        for odd in range(2):
-            cols = slice(odd * T, (odd + 1) * T)
-            flat = jnp.concatenate([t[:, cols] for t in both], axis=1)
-            base[2 * p + odd] = sum(dot(part, ht[odd, pl.ds(T, 2 * T)]) for part in split(flat, 2))
-
-    for item in fars:
-        arrived(item)
-    q = []
-    for p in range(2):
-        v_side = sum(dot(vm[pl.ds(0, T)], part) for part in split(side(p, pl.ds(0, E), low_all), 3))
-        q += [pooled(0, p, odd, v_side) for odd in range(2)]
-    slopes(0, q)
+    late = [[], [], []]
+    for p in range(2):
+        v_side = dot(vl[...], jnp.concatenate(split(side(p, to_outer, low_pad), 3), axis=0))
+        for i in range(3):
+            share = along_rows(v_side[begins[i] : begins[i] + sizes[i]], 1, i)
+            late[i].append(qs[i, p, rows(touched[i], sizes[i])] + share)
+    for i in range(3):
+        slopes(i, touched[i], late[i])
 
     def piece(p, half):
-        high = tall(0, p, half)
+        high = [dot(vt[i, half], sig[i, :, pl.ds(2 * p * T, 2 * T)]) for i in range(3)]
         frame = []
         for odd in range(2):
-            cols = slice(odd * T, (odd + 1) * T)
-            full = base[2 * p + odd, half] + sum(
-                dot(part, ht[odd, pl.ds(0, T)]) for part in split(high[:, cols], 2)
-            )
+            flat = jnp.concatenate([t[:, odd * T : (odd + 1) * T] for t in high], axis=1)
+            full = dot(jnp.concatenate(split(flat, 2), axis=1), ht[odd])
             own2[2 * p + odd, half] = full[:, :T]
             frame.append(full[:, T:])
         s_r[p, half] = jnp.where(low, frame[0], frame[1])
@@ -324,16 +325,16 @@
             vmem((4, T, T), F32), vmem((T, T), F32), vmem((T, T), jnp.int32),
             vmem((4, E, T), F32), vmem((2, E, T), F32), vmem((2, E, T), F32),
             vmem((2, T, T), F32), vmem((2, T, T), F32),
-            vmem((3 * T, E), BF16), vmem((2 * T, MID), BF16), vmem((3, E, T), BF16),
-            vmem((2, 3, E, T), BF16), vmem((2, 3 * T, E), BF16),
-            vmem((2, 3, T, 4 * T), BF16), vmem((4, E, E), F32),
+            vmem((3 * T, 3 * E), BF16), vmem((3 * T, 3 * REST), BF16), vmem((LATE, 3 * PAD), BF16),
+            vmem((3, E, 2 * T), BF16), vmem((2, 3, E, 2 * T), BF16), vmem((2, 6 * T, E), BF16),
+            vmem((3, 2 * T, 4 * T), BF16), vmem((3, 2, T, 2 * T), F32),
             vmem((4, E, T), F32), vmem((2, E, T), F32), vmem((2, E, T), F32),
             vmem((2, PAD, T), F32), vmem((2, PAD, T), F32),
             vmem((4, T, T), F32),
             vmem((2, T, T), F32), vmem((2, T, T), F32), vmem((2, T, T), F32), vmem((2, T, T), F32),
             pltpu.SemaphoreType.DMA((3,)),
             pltpu.SemaphoreType.DMA((40,)), pltpu.SemaphoreType.DMA((40,)),
-            pltpu.SemaphoreType.REGULAR((2,)),
+            pltpu.SemaphoreType.REGULAR,
         ],
         compiler_params=pltpu.CompilerParams(
             collective_id=0, has_side_effects=True, vmem_limit_bytes=40 * 1024 * 1024

time: 22.9 us -> 22.2 us (0.969)
  the two profiles are of different devices: /device:TPU:99 before, /device:TPU:199 now
where the time goes in v4:
time: 22.2 us; the launch traced here: 22.1 us
  Pallas kernels  21.4 us (96%)
  local copies, waits for them, and re-layouts  0.71 us (3%)
    pallas_call x1, Pallas kernels, local(): pl.pallas_call(kernel, out_shape=jax.ShapeDtypeStruct((4, T, T), F32), in...  21.4 us
    unnamed x1, local copies, waits for them, and re-layouts  0.71 us

profile of v4, /device:TPU:199, one launch (start us, length us, event | category | flops | bytes accessed | tf_op | source)
XLA Modules:
  0.0 22.1 jit_solution(8658036270990649057)
XLA Ops:
  0.0 21.4 %shard_map.37 = f32[4,128,128]{2,1,0:T(8,128)S(1)} custom-call(f32[4,128,128]{2,1,0:T(8,128)} %mem_hbm.1, f32[128,128]{1,0:T(8,128)} %ana_hbm.1, s32[128,128]{1,0:T(8,128)} %land_hbm.1), custom_call_target="tpu_custom_call" | custom-call | tf_op jit(solution)/shard_map/pallas_call | solution.py:319
  21.4 0.7 %copy.5 = f32[4,128,128]{2,1,0:T(8,128)} copy(f32[4,128,128]{2,1,0:T(8,128)S(1)} %shard_map.37) | data formatting | bytes 524288

commit v5 on v4

--- a/solution.py
+++ b/solution.py
@@ -158,9 +158,9 @@
 
     tell(ok, "o", has_o)
     mains = []
-    for p in range(2):
-        mains.append(send("l", go_l.at[p], rgt.at[p, body]))
-        mains.append(send("r", go_r.at[p], lft.at[p, body]))
+    for part, there in ((near_mate, inner_src), (near_outer, outer_src)):
+        mains.append(send("l", go_l.at[:, part], rgt.at[:, there]))
+        mains.append(send("r", go_r.at[:, part], lft.at[:, there]))
     to_o = send("o", ctr.at[:, outer_src], ctr.at[:, outer_dst])
     to_m = send("m", ctr.at[:, inner_src], ctr.at[:, inner_dst])
 
@@ -219,13 +219,12 @@
         for i in range(3):
             qs[i, p] = along_rows(v_own[i * T : (i + 1) * T], 0, i)
 
-    forwards = []
-    for p in range(2):
-        arrived(mains[2 * p])
-        arrived(mains[2 * p + 1])
-        forwards.append(send("m", lft.at[p, inner_src], lft.at[p, inner_dst], has_l))
-        forwards.append(send("m", rgt.at[p, inner_src], rgt.at[p, inner_dst], has_r))
-
+    arrived(mains[0])
+    arrived(mains[1])
+    forwards = [
+        send("m", lft.at[:, inner_src], lft.at[:, inner_dst], has_l),
+        send("m", rgt.at[:, inner_src], rgt.at[:, inner_dst], has_r),
+    ]
     loads[2].wait()
 
     def side(p, part, mask):
@@ -249,9 +248,9 @@
             for h, piece in enumerate(split(value, 2)):
                 sig[i, rows(h * T + start, size), pl.ds(j * T, T)] = piece
 
-    for p in range(2):
-        arrived(forwards[2 * p])
-        arrived(forwards[2 * p + 1])
+    for item in mains[2:] + forwards:
+        arrived(item)
+    for p in range(2):
         v_side = dot(ve[...], jnp.concatenate(split(side(p, rest, low_rest), 3), axis=0))
         for i in range(3):
             qs[i, p] = qs[i, p] + along_rows(v_side[i * T : (i + 1) * T], 1, i)
@@ -281,27 +280,30 @@
         s_l[p, half] = jnp.where(low, frame[1], frame[0])
 
     second, give = [], []
-    for p in range(2):
+    for p in (0,):
         piece(p, outer_half)
-        both = pl.ds(2 * p, 2)
         second.append(send("ol", s_l.at[p, to_outer], k_r.at[p, outers_near]))
         second.append(send("or", s_r.at[p, to_outer], k_l.at[p, outers_near]))
         second.append(send("l", s_l.at[p, outer_src], in_r.at[p, near_outer]))
         second.append(send("r", s_r.at[p, outer_src], in_l.at[p, near_outer]))
-        second.append(send("o", own2.at[both, to_outer], ud.at[both, outers_near]))
+    for p in (1,):
+        piece(p, outer_half)
+        second.append(send("ol", s_l.at[p, to_outer], k_r.at[p, outers_near]))
+        second.append(send("or", s_r.at[p, to_outer], k_l.at[p, outers_near]))
+        second.append(send("l", s_l.at[p, outer_src], in_r.at[p, near_outer]))
+        second.append(send("r", s_r.at[p, outer_src], in_l.at[p, near_outer]))
     for p in range(2):
         piece(p, inner_half)
-        both = pl.ds(2 * p, 2)
-        give.append(send("m", s_r.at[p, to_mate], q_r.at[p]))
-        give.append(send("m", s_l.at[p, to_mate], q_l.at[p]))
-        second.append(send("m", own2.at[both, to_mate], ud.at[both, mates_near]))
-    for p in range(2):
-        arrived(give[2 * p])
-        arrived(give[2 * p + 1])
-        s_r[p, inner_src] = s_r[p, inner_src] + q_r[p]
-        s_l[p, inner_src] = s_l[p, inner_src] + q_l[p]
-        second.append(send("l", s_l.at[p, inner_src], in_r.at[p, near_mate]))
-        second.append(send("r", s_r.at[p, inner_src], in_l.at[p, near_mate]))
+    give.append(send("m", s_r.at[:, to_mate], q_r))
+    give.append(send("m", s_l.at[:, to_mate], q_l))
+    arrived(give[0])
+    arrived(give[1])
+    s_r[:, inner_src] = s_r[:, inner_src] + q_r[...]
+    s_l[:, inner_src] = s_l[:, inner_src] + q_l[...]
+    second.append(send("l", s_l.at[:, inner_src], in_r.at[:, near_mate]))
+    second.append(send("r", s_r.at[:, inner_src], in_l.at[:, near_mate]))
+    second.append(send("o", own2.at[:, to_outer], ud.at[:, outers_near]))
+    second.append(send("m", own2.at[:, to_mate], ud.at[:, mates_near]))
 
     for item in second:
         arrived(item)

time: 22.2 us -> 21.6 us (0.973)
  the two profiles are of different devices: /device:TPU:199 before, /device:TPU:99 now
where the time goes in v5:
time: 21.6 us; the launch traced here: 21.4 us
  Pallas kernels  20.7 us (96%)
  local copies, waits for them, and re-layouts  0.71 us (3%)
    pallas_call x1, Pallas kernels, local(): pl.pallas_call(kernel, out_shape=jax.ShapeDtypeStruct((4, T, T), F32), in...  20.7 us
    unnamed x1, local copies, waits for them, and re-layouts  0.71 us

profile of v5, /device:TPU:99, one launch (start us, length us, event | category | flops | bytes accessed | tf_op | source)
XLA Modules:
  0.0 21.4 jit_solution(2259602342181286399)
XLA Ops:
  0.0 20.7 %shard_map.37 = f32[4,128,128]{2,1,0:T(8,128)S(1)} custom-call(f32[4,128,128]{2,1,0:T(8,128)} %mem_hbm.1, f32[128,128]{1,0:T(8,128)} %ana_hbm.1, s32[128,128]{1,0:T(8,128)} %land_hbm.1), custom_call_target="tpu_custom_call" | custom-call | tf_op jit(solution)/shard_map/pallas_call | solution.py:321
  20.7 0.7 %copy.5 = f32[4,128,128]{2,1,0:T(8,128)} copy(f32[4,128,128]{2,1,0:T(8,128)S(1)} %shard_map.37) | data formatting | bytes 524288

commit v6 on v5

--- a/solution.py
+++ b/solution.py
@@ -132,8 +132,19 @@
         sent.append((here, copy))
         return there, copy
 
-    def arrived(item):
-        when(item[0], item[1].wait_recv)
+    def grouped(pairs):
+        groups = {}
+        for cond, wait in pairs:
+            groups.setdefault(id(cond), (cond, []))[1].append(wait)
+        for cond, waits in groups.values():
+            when(cond, lambda waits=waits: [wait() for wait in waits] and None)
+
+    def arrived(*items):
+        grouped([(there, copy.wait_recv) for there, copy in items])
+
+    def flush():
+        grouped([(here, copy.wait_send) for here, copy in sent])
+        sent.clear()
 
     def fill(cond, ref, part=None):
         def zero():
@@ -206,21 +217,22 @@
             for h in range(2):
                 ht[odd, pl.ds((3 * h + i) * T, T)] = jnp.concatenate([square, back[odd]], axis=1)
 
-    def along_rows(pair, first, i):
-        size = pair.shape[0]
-        out = dot(jnp.concatenate(split(pair, 3), axis=0), hm[first, i])
-        return out[:size] + out[size : 2 * size] + out[2 * size :]
-
-    arrived(to_m)
-    arrived(to_o)
+    def along_rows(pairs, first, i):
+        size = pairs[0].shape[0]
+        out = dot(jnp.concatenate([term for pair in pairs for term in split(pair, 3)], axis=0), hm[first, i])
+        out = [out[k * size : (k + 1) * size] for k in range(3 * len(pairs))]
+        return [out[3 * k] + out[3 * k + 1] + out[3 * k + 2] for k in range(len(pairs))]
+
+    arrived(to_m, to_o)
+    v_own = []
     for p in range(2):
         wide = jnp.concatenate([ctr[2 * p], ctr[2 * p + 1]], axis=1)
-        v_own = dot(vm[...], jnp.concatenate(split(wide, 3), axis=0))
-        for i in range(3):
-            qs[i, p] = along_rows(v_own[i * T : (i + 1) * T], 0, i)
-
-    arrived(mains[0])
-    arrived(mains[1])
+        v_own.append(dot(vm[...], jnp.concatenate(split(wide, 3), axis=0)))
+    for i in range(3):
+        for p, out in enumerate(along_rows([v[i * T : (i + 1) * T] for v in v_own], 0, i)):
+            qs[i, p] = out
+
+    arrived(*mains[:2])
     forwards = [
         send("m", lft.at[:, inner_src], lft.at[:, inner_dst], has_l),
         send("m", rgt.at[:, inner_src], rgt.at[:, inner_dst], has_r),
@@ -248,56 +260,53 @@
             for h, piece in enumerate(split(value, 2)):
                 sig[i, rows(h * T + start, size), pl.ds(j * T, T)] = piece
 
-    for item in mains[2:] + forwards:
-        arrived(item)
-    for p in range(2):
-        v_side = dot(ve[...], jnp.concatenate(split(side(p, rest, low_rest), 3), axis=0))
-        for i in range(3):
-            qs[i, p] = qs[i, p] + along_rows(v_side[i * T : (i + 1) * T], 1, i)
+    arrived(*mains[2:], *forwards)
+    v_side = [
+        dot(ve[...], jnp.concatenate(split(side(p, rest, low_rest), 3), axis=0)) for p in range(2)
+    ]
+    for i in range(3):
+        for p, out in enumerate(along_rows([v[i * T : (i + 1) * T] for v in v_side], 1, i)):
+            qs[i, p] = qs[i, p] + out
     for i in range(3):
         slopes(i, apart[i], [qs[i, p, rows(apart[i], T - sizes[i])] for p in range(2)])
 
-    for item in corners:
-        arrived(item)
-    late = [[], [], []]
+    arrived(*corners)
+    v_side = [
+        dot(vl[...], jnp.concatenate(split(side(p, to_outer, low_pad), 3), axis=0)) for p in range(2)
+    ]
+    for i in range(3):
+        share = along_rows([v[begins[i] : begins[i] + sizes[i]] for v in v_side], 1, i)
+        slopes(i, touched[i], [qs[i, p, rows(touched[i], sizes[i])] + share[p] for p in range(2)])
+
+    def piece(todo):
+        flat = [[], []]
+        for p, half in todo:
+            high = [dot(vt[i, half], sig[i, :, pl.ds(2 * p * T, 2 * T)]) for i in range(3)]
+            for odd in range(2):
+                one = jnp.concatenate([t[:, odd * T : (odd + 1) * T] for t in high], axis=1)
+                flat[odd].append(jnp.concatenate(split(one, 2), axis=1))
+        full = [dot(jnp.concatenate(flat[odd], axis=0), ht[odd]) for odd in range(2)]
+        for k, (p, half) in enumerate(todo):
+            block = slice(k * T, (k + 1) * T)
+            for odd in range(2):
+                own2[2 * p + odd, half] = full[odd][block, :T]
+            frame = [full[odd][block, T:] for odd in range(2)]
+            s_r[p, half] = jnp.where(low, frame[0], frame[1])
+            s_l[p, half] = jnp.where(low, frame[1], frame[0])
+
+    old = [(here, copy.wait_send) for here, copy in sent]
+    sent.clear()
+    second, give = [], []
+    todo = ([(0, outer_half)], [(1, outer_half), (0, inner_half), (1, inner_half)])
     for p in range(2):
-        v_side = dot(vl[...], jnp.concatenate(split(side(p, to_outer, low_pad), 3), axis=0))
-        for i in range(3):
-            share = along_rows(v_side[begins[i] : begins[i] + sizes[i]], 1, i)
-            late[i].append(qs[i, p, rows(touched[i], sizes[i])] + share)
-    for i in range(3):
-        slopes(i, touched[i], late[i])
-
-    def piece(p, half):
-        high = [dot(vt[i, half], sig[i, :, pl.ds(2 * p * T, 2 * T)]) for i in range(3)]
-        frame = []
-        for odd in range(2):
-            flat = jnp.concatenate([t[:, odd * T : (odd + 1) * T] for t in high], axis=1)
-            full = dot(jnp.concatenate(split(flat, 2), axis=1), ht[odd])
-            own2[2 * p + odd, half] = full[:, :T]
-            frame.append(full[:, T:])
-        s_r[p, half] = jnp.where(low, frame[0], frame[1])
-        s_l[p, half] = jnp.where(low, frame[1], frame[0])
-
-    second, give = [], []
-    for p in (0,):
-        piece(p, outer_half)
+        piece(todo[p])
         second.append(send("ol", s_l.at[p, to_outer], k_r.at[p, outers_near]))
         second.append(send("or", s_r.at[p, to_outer], k_l.at[p, outers_near]))
         second.append(send("l", s_l.at[p, outer_src], in_r.at[p, near_outer]))
         second.append(send("r", s_r.at[p, outer_src], in_l.at[p, near_outer]))
-    for p in (1,):
-        piece(p, outer_half)
-        second.append(send("ol", s_l.at[p, to_outer], k_r.at[p, outers_near]))
-        second.append(send("or", s_r.at[p, to_outer], k_l.at[p, outers_near]))
-        second.append(send("l", s_l.at[p, outer_src], in_r.at[p, near_outer]))
-        second.append(send("r", s_r.at[p, outer_src], in_l.at[p, near_outer]))
-    for p in range(2):
-        piece(p, inner_half)
     give.append(send("m", s_r.at[:, to_mate], q_r))
     give.append(send("m", s_l.at[:, to_mate], q_l))
-    arrived(give[0])
-    arrived(give[1])
+    arrived(*give)
     s_r[:, inner_src] = s_r[:, inner_src] + q_r[...]
     s_l[:, inner_src] = s_l[:, inner_src] + q_l[...]
     second.append(send("l", s_l.at[:, inner_src], in_r.at[:, near_mate]))
@@ -305,15 +314,14 @@
     second.append(send("o", own2.at[:, to_outer], ud.at[:, outers_near]))
     second.append(send("m", own2.at[:, to_mate], ud.at[:, mates_near]))
 
-    for item in second:
-        arrived(item)
+    grouped(old)
+    arrived(*second)
     for p in range(2):
         a, b = in_l[p] + k_l[p], in_r[p] + k_r[p]
         e, o = 2 * p, 2 * p + 1
         out_ref[e] = own2[e, body] + ud[e] + jnp.where(low, a, b)
         out_ref[o] = own2[o, body] + ud[o] + pltpu.roll(jnp.where(low, b, a), PAD, 1)
-    for here, copy in sent:
-        when(here, copy.wait_send)
+    flush()
 
 
 def local(members, analysis, land_sea):

time: 21.6 us -> 21.1 us (0.977)
  Pallas kernels: 20.7 us -> 20 us
    pallas_call x1, Pallas kernels: 20.7 us -> 20 us  [local(): pl.pallas_call(kernel, out_shape=jax.ShapeDtypeStruct((4, T, T), F32), in...]
where the time goes in v6:
time: 21.1 us; the launch traced here: 20.8 us
  Pallas kernels  20 us (95%)
  local copies, waits for them, and re-layouts  0.71 us (3%)
    pallas_call x1, Pallas kernels, local(): pl.pallas_call(kernel, out_shape=jax.ShapeDtypeStruct((4, T, T), F32), in...  20 us
    unnamed x1, local copies, waits for them, and re-layouts  0.71 us

profile of v6, /device:TPU:99, one launch (start us, length us, event | category | flops | bytes accessed | tf_op | source)
XLA Modules:
  0.0 20.8 jit_solution(16303007313229084972)
XLA Ops:
  0.0 20.0 %shard_map.37 = f32[4,128,128]{2,1,0:T(8,128)S(1)} custom-call(f32[4,128,128]{2,1,0:T(8,128)} %mem_hbm.1, f32[128,128]{1,0:T(8,128)} %ana_hbm.1, s32[128,128]{1,0:T(8,128)} %land_hbm.1), custom_call_target="tpu_custom_call" | custom-call | tf_op jit(solution)/shard_map/pallas_call | solution.py:329
  20.0 0.7 %copy.5 = f32[4,128,128]{2,1,0:T(8,128)} copy(f32[4,128,128]{2,1,0:T(8,128)S(1)} %shard_map.37) | data formatting | bytes 524288

commit v7 on v6

--- a/solution.py
+++ b/solution.py
@@ -223,6 +223,12 @@
         out = [out[k * size : (k + 1) * size] for k in range(3 * len(pairs))]
         return [out[3 * k] + out[3 * k + 1] + out[3 * k + 2] for k in range(len(pairs))]
 
+    arrived(*mains[:2])
+    forwards = [
+        send("m", lft.at[:, inner_src], lft.at[:, inner_dst], has_l),
+        send("m", rgt.at[:, inner_src], rgt.at[:, inner_dst], has_r),
+    ]
+
     arrived(to_m, to_o)
     v_own = []
     for p in range(2):
@@ -232,11 +238,6 @@
         for p, out in enumerate(along_rows([v[i * T : (i + 1) * T] for v in v_own], 0, i)):
             qs[i, p] = out
 
-    arrived(*mains[:2])
-    forwards = [
-        send("m", lft.at[:, inner_src], lft.at[:, inner_dst], has_l),
-        send("m", rgt.at[:, inner_src], rgt.at[:, inner_dst], has_r),
-    ]
     loads[2].wait()
 
     def side(p, part, mask):

time: 21.1 us -> 20.8 us (0.986)
  Pallas kernels: 20 us -> 19.7 us
    pallas_call x1, Pallas kernels: 20 us -> 19.7 us  [local(): pl.pallas_call(kernel, out_shape=jax.ShapeDtypeStruct((4, T, T), F32), in...]
where the time goes in v7:
time: 20.8 us; the launch traced here: 20.4 us
  Pallas kernels  19.7 us (95%)
  local copies, waits for them, and re-layouts  0.71 us (3%)
    pallas_call x1, Pallas kernels, local(): pl.pallas_call(kernel, out_shape=jax.ShapeDtypeStruct((4, T, T), F32), in...  19.7 us
    unnamed x1, local copies, waits for them, and re-layouts  0.71 us

profile of v7, /device:TPU:99, one launch (start us, length us, event | category | flops | bytes accessed | tf_op | source)
XLA Modules:
  0.0 20.4 jit_solution(11411682913576184544)
XLA Ops:
  0.0 19.7 %shard_map.37 = f32[4,128,128]{2,1,0:T(8,128)S(1)} custom-call(f32[4,128,128]{2,1,0:T(8,128)} %mem_hbm.1, f32[128,128]{1,0:T(8,128)} %ana_hbm.1, s32[128,128]{1,0:T(8,128)} %land_hbm.1), custom_call_target="tpu_custom_call" | custom-call | tf_op jit(solution)/shard_map/pallas_call | solution.py:330
  19.7 0.7 %copy.5 = f32[4,128,128]{2,1,0:T(8,128)} copy(f32[4,128,128]{2,1,0:T(8,128)S(1)} %shard_map.37) | data formatting | bytes 524288

commit v8 on v7

--- a/solution.py
+++ b/solution.py
@@ -87,9 +87,9 @@
         tell(barrier, name, to[name])
 
     loads = [
-        pltpu.make_async_copy(mem_hbm, mem, in_sem.at[0]),
-        pltpu.make_async_copy(ana_hbm, ana, in_sem.at[1]),
-        pltpu.make_async_copy(land_hbm, land, in_sem.at[2]),
+        *(pltpu.make_async_copy(mem_hbm.at[m], mem.at[m], in_sem.at[m]) for m in range(4)),
+        pltpu.make_async_copy(ana_hbm, ana, in_sem.at[4]),
+        pltpu.make_async_copy(land_hbm, land, in_sem.at[5]),
     ]
     for load in loads:
         load.start()
@@ -154,8 +154,8 @@
                 ref[:, part, :] = jnp.zeros((ref.shape[0], PAD, T), ref.dtype)
         pl.when(cond)(zero)
 
-    loads[0].wait()
-    loads[1].wait()
+    for load in loads[:5]:
+        load.wait()
     for m in range(4):
         ctr[m, body] = mem[m] - ana[...]
     for p in range(2):
@@ -238,7 +238,7 @@
         for p, out in enumerate(along_rows([v[i * T : (i + 1) * T] for v in v_own], 0, i)):
             qs[i, p] = out
 
-    loads[2].wait()
+    loads[5].wait()
 
     def side(p, part, mask):
         a, b = lft[p, part], rgt[p, part]
@@ -343,7 +343,7 @@
             vmem((2, PAD, T), F32), vmem((2, PAD, T), F32),
             vmem((4, T, T), F32),
             vmem((2, T, T), F32), vmem((2, T, T), F32), vmem((2, T, T), F32), vmem((2, T, T), F32),
-            pltpu.SemaphoreType.DMA((3,)),
+            pltpu.SemaphoreType.DMA((6,)),
             pltpu.SemaphoreType.DMA((40,)), pltpu.SemaphoreType.DMA((40,)),
             pltpu.SemaphoreType.REGULAR,
         ],

time: 20.8 us -> 20.8 us (level)
  the two profiles are of different devices: /device:TPU:99 before, /device:TPU:167 now
where the time goes in v8:
time: 20.8 us; the launch traced here: 20.7 us
  Pallas kernels  20 us (96%)
  local copies, waits for them, and re-layouts  0.71 us (3%)
    pallas_call x1, Pallas kernels, local(): pl.pallas_call(kernel, out_shape=jax.ShapeDtypeStruct((4, T, T), F32), in...  20 us
    unnamed x1, local copies, waits for them, and re-layouts  0.71 us

profile of v8, /device:TPU:167, one launch (start us, length us, event | category | flops | bytes accessed | tf_op | source)
XLA Modules:
  0.0 20.7 jit_solution(1134246053501977797)
XLA Ops:
  0.0 20.0 %shard_map.37 = f32[4,128,128]{2,1,0:T(8,128)S(1)} custom-call(f32[4,128,128]{2,1,0:T(8,128)} %mem_hbm.1, f32[128,128]{1,0:T(8,128)} %ana_hbm.1, s32[128,128]{1,0:T(8,128)} %land_hbm.1), custom_call_target="tpu_custom_call" | custom-call | tf_op jit(solution)/shard_map/pallas_call | solution.py:330
  20.0 0.7 %copy.5 = f32[4,128,128]{2,1,0:T(8,128)} copy(f32[4,128,128]{2,1,0:T(8,128)S(1)} %shard_map.37) | data formatting | bytes 524288

commit v9 on v7

--- a/solution.py
+++ b/solution.py
@@ -82,10 +82,6 @@
             pl.semaphore_signal(semaphore, inc=1, device_id=dev[name], device_id_type=MESH)
         when(cond, signal)
 
-    barrier = pltpu.get_barrier_semaphore()
-    for name in ("l", "r", "o", "m"):
-        tell(barrier, name, to[name])
-
     loads = [
         pltpu.make_async_copy(mem_hbm, mem, in_sem.at[0]),
         pltpu.make_async_copy(ana_hbm, ana, in_sem.at[1]),
@@ -93,6 +89,10 @@
     ]
     for load in loads:
         load.start()
+
+    barrier = pltpu.get_barrier_semaphore()
+    for name in ("l", "r", "o", "m"):
+        tell(barrier, name, to[name])
 
     def rows(start, size=PAD):
         return pl.ds(pl.multiple_of(start, NEAR), size)

time: 20.8 us -> 20.8 us (level)
  no operation moved by 1% of the time
where the time goes in v9:
time: 20.8 us; the launch traced here: 20.4 us
  Pallas kernels  19.7 us (95%)
  local copies, waits for them, and re-layouts  0.71 us (3%)
    pallas_call x1, Pallas kernels, local(): pl.pallas_call(kernel, out_shape=jax.ShapeDtypeStruct((4, T, T), F32), in...  19.7 us
    unnamed x1, local copies, waits for them, and re-layouts  0.71 us

profile of v9, /device:TPU:99, one launch (start us, length us, event | category | flops | bytes accessed | tf_op | source)
XLA Modules:
  0.0 20.4 jit_solution(6555602012115655805)
XLA Ops:
  0.0 19.7 %shard_map.37 = f32[4,128,128]{2,1,0:T(8,128)S(1)} custom-call(f32[4,128,128]{2,1,0:T(8,128)} %mem_hbm.1, f32[128,128]{1,0:T(8,128)} %ana_hbm.1, s32[128,128]{1,0:T(8,128)} %land_hbm.1), custom_call_target="tpu_custom_call" | custom-call | tf_op jit(solution)/shard_map/pallas_call | solution.py:330
  19.7 0.7 %copy.5 = f32[4,128,128]{2,1,0:T(8,128)} copy(f32[4,128,128]{2,1,0:T(8,128)S(1)} %shard_map.37) | data formatting | bytes 524288
